TPU v7x, 32 devices: a whole 2x2x4 slice. The times are simulated.
32 devices in a mesh: ia: 8 (over z, core), ja: 4 (over y, x).
Axes of the slice: x: 2, y: 2, z: 4, core: 2. Of those that a mesh axis runs over, the one named last changes fastest.
Arguments:
- slab_rows: bfloat16 [256, 96, 128], P('ia', 'ja'), may hold values from -6 to 6
- column_rows: bfloat16 [64, 96, 128], P('ja', 'ia'), may hold values from -6 to 6
- pair_tile: bfloat16 [256, 64, 128], P('ia', 'ja'), may hold values from -6 to 6
- cotangent: bfloat16 [256, 64, 128], P('ia', 'ja'), may hold values from -6 to 6
- weights_left: bfloat16 [128, 256], replicated, may hold values from -0.5 to 0.5
- weights_right: bfloat16 [128, 256], replicated, may hold values from -0.5 to 0.5
- gate_weight: bfloat16 [128, 128], replicated, may hold values from -0.5 to 0.5
- out_weight: bfloat16 [128, 128], replicated, may hold values from -0.5 to 0.5
- input_gain: float32 [128], replicated, may hold values from 0.1 to 1.9
- input_bias: float32 [128], replicated, may hold values from -3 to 3
- update_gain: float32 [128], replicated, may hold values from 0.1 to 1.9
- update_bias: float32 [128], replicated, may hold values from -3 to 3
Outputs:
- update: bfloat16 [256, 64, 128], P('ia', 'ja')
- grad_slab: bfloat16 [256, 96, 128], P('ia', 'ja')
- grad_columns: bfloat16 [64, 96, 128], P('ja', 'ia')
- grad_tile: bfloat16 [256, 64, 128], P('ia', 'ja')
All inputs are finite; a program needn't handle non-finite values.
Results may differ from a plain program's by a relative error of at most 0.018.
Values may be sent and summed in bfloat16 or wider, within the bound.
A program may use at most 128 MiB of HBM per device.

v0:
```python
import jax
import jax.numpy as jnp
from jax import lax
from jax.sharding import PartitionSpec as P

epsilon = 1e-05


def normalize(values, gain, bias):
    values = values.astype(jnp.float32)
    centre = jnp.mean(values, axis=-1, keepdims=True)
    shifted = values - centre
    inverse = lax.rsqrt(jnp.mean(shifted * shifted, axis=-1, keepdims=True) + epsilon)
    scaled = shifted * inverse
    return (scaled * gain + bias, scaled, inverse)


def norm_back(scaled, inverse, grad_out, gain):
    grad_hat = grad_out * gain
    first_mean = jnp.mean(grad_hat, axis=-1, keepdims=True)
    second_mean = jnp.mean(grad_hat * scaled, axis=-1, keepdims=True)
    return inverse * (grad_hat - first_mean - scaled * second_mean)


def project(rows, weights, input_gain, input_bias):
    normed, scaled, inverse = normalize(rows, input_gain, input_bias)
    hidden = jnp.dot(normed.astype(jnp.bfloat16), weights, preferred_element_type=jnp.float32)
    half_width = weights.shape[1] // 2
    linear = hidden[..., :half_width]
    sigma = jax.nn.sigmoid(hidden[..., half_width:])
    return ((sigma * linear).astype(jnp.bfloat16), linear, sigma, scaled, inverse)


def project_back(grad_edge, linear, sigma, scaled, inverse, weights, input_gain):
    joined = jnp.concatenate(
        [grad_edge * sigma, grad_edge * linear * sigma * (1.0 - sigma)], axis=-1
    )
    grad_norm = jnp.dot(joined.astype(jnp.bfloat16), weights.T, preferred_element_type=jnp.float32)
    return norm_back(scaled, inverse, grad_norm, input_gain).astype(jnp.bfloat16)


def shards(
    slab_rows,
    column_rows,
    pair_tile,
    cotangent,
    weights_left,
    weights_right,
    gate_weight,
    out_weight,
    input_gain,
    input_bias,
    update_gain,
    update_bias,
):
    left, lin_left, sig_left, scaled_left, inv_left = project(
        slab_rows, weights_left, input_gain, input_bias
    )
    right, lin_right, sig_right, scaled_right, inv_right = project(
        column_rows, weights_right, input_gain, input_bias
    )
    left_whole = lax.all_gather(left, "ja", axis=1, tiled=True)
    panel_piece = lax.all_gather(right, "ia", axis=1, tiled=True)
    left_slice = left_whole
    running = jnp.einsum(
        "ikc,jkc->ijc", left_slice, panel_piece, preferred_element_type=jnp.float32
    )
    tri_norm, tri_scaled, tri_inverse = normalize(running, update_gain, update_bias)
    outer = jnp.dot(tri_norm.astype(jnp.bfloat16), out_weight, preferred_element_type=jnp.float32)
    tile_norm, tile_scaled, tile_inverse = normalize(pair_tile, input_gain, input_bias)
    gate_linear = jnp.dot(
        tile_norm.astype(jnp.bfloat16), gate_weight, preferred_element_type=jnp.float32
    )
    gate = jax.nn.sigmoid(gate_linear)
    update = (gate * outer).astype(jnp.bfloat16)
    grad_update = cotangent.astype(jnp.float32)
    grad_outer = (grad_update * gate).astype(jnp.bfloat16)
    grad_gate = (grad_update * outer * gate * (1.0 - gate)).astype(jnp.bfloat16)
    grad_tnorm = jnp.dot(grad_outer, out_weight.T, preferred_element_type=jnp.float32)
    grad_tri = norm_back(tri_scaled, tri_inverse, grad_tnorm, update_gain).astype(jnp.bfloat16)
    grad_pnorm = jnp.dot(grad_gate, gate_weight.T, preferred_element_type=jnp.float32)
    grad_tile = norm_back(tile_scaled, tile_inverse, grad_pnorm, input_gain).astype(jnp.bfloat16)
    left_sums = lax.psum_scatter(
        jnp.einsum(
            "ijc,jkc->kic", grad_tri, panel_piece, preferred_element_type=jnp.float32
        ).astype(jnp.bfloat16),
        "ja",
        scatter_dimension=0,
        tiled=True,
    ).astype(jnp.float32)
    left_slice = left_whole
    right_sums = lax.psum_scatter(
        jnp.einsum("ijc,ikc->kjc", grad_tri, left_slice, preferred_element_type=jnp.float32).astype(
            jnp.bfloat16
        ),
        "ia",
        scatter_dimension=0,
        tiled=True,
    ).astype(jnp.float32)
    grad_left = jnp.transpose(left_sums, (1, 0, 2))
    grad_right = jnp.transpose(right_sums, (1, 0, 2))
    grad_slab = project_back(
        grad_left, lin_left, sig_left, scaled_left, inv_left, weights_left, input_gain
    )
    grad_columns = project_back(
        grad_right, lin_right, sig_right, scaled_right, inv_right, weights_right, input_gain
    )
    return (update, grad_slab, grad_columns, grad_tile)


def solution(mesh):
    return jax.shard_map(
        shards,
        mesh=mesh,
        in_specs=(
            P("ia", "ja", None),
            P("ja", "ia", None),
            P("ia", "ja", None),
            P("ia", "ja", None),
            P(),
            P(),
            P(),
            P(),
            P(),
            P(),
            P(),
            P(),
        ),
        out_specs=(
            P("ia", "ja", None),
            P("ia", "ja", None),
            P("ja", "ia", None),
            P("ia", "ja", None),
        ),
        check_vma=False,
    )
```

profile of v0, /device:TPU:0, one launch (start us, length us, event | category | flops | bytes accessed | tf_op | source)
XLA Modules:
  0.0 139.1 jit_solution(256588015776704546)
XLA Ops:
  8.1 1.1 convert_reduce_fusion
  9.2 1.2 fusion.15
  11.0 1.4 fusion.42
  13.3 16.3 %all_gather.7 = bf16[32,96,128]{2,1,0:T(8,128)(2,1)} all-gather(bf16[32,24,128]{2,1,0:T(8,128)(2,1)S(1)} %multiply_convert_fusion.1), channel_id=1, replica_groups=mesh['ia'=8,'ja'=4] {'ja'}, dimensions={1}, use_global_device_ids=true | all-gather | bytes 983040 | tf_op jit(solution)/shard_map/all_gather | solution.py:62
  29.6 6.2 %copy.61 = bf16[32,96,128]{0,1,2:T(8,128)(2,1)S(1)} copy(bf16[32,96,128]{2,1,0:T(8,128)(2,1)} %all_gather.7) | data formatting | bytes 1572864 | tf_op jit(solution)/shard_map/all_gather | solution.py:62
  37.2 15.8 %all_gather.6 = bf16[16,96,128]{2,0,1:T(8,128)(2,1)} all-gather(bf16[16,12,128]{2,0,1:T(8,128)(2,1)S(1)} %multiply_convert_fusion.3), channel_id=1, replica_groups=mesh['ia'=8,'ja'=4] {'ia'}, dimensions={1}, use_global_device_ids=true | all-gather | bytes 442368 | tf_op jit(solution)/shard_map/all_gather | solution.py:63
  53.0 2.4 %copy.60 = bf16[16,96,128]{1,0,2:T(8,128)(2,1)} copy(bf16[16,96,128]{2,0,1:T(8,128)(2,1)} %all_gather.6) | data formatting | bytes 786432 | tf_op jit(solution)/shard_map/all_gather | solution.py:63
  55.4 2.0 %fusion.100 = (f32[32,16]{0,1:T(8,128)S(1)}, f32[32,16,128]{0,1,2:T(8,128)S(1)}) fusion(bf16[16,96,128]{1,0,2:T(8,128)(2,1)} %copy.60, bf16[32,96,128]{0,1,2:T(8,128)(2,1)S(1)} %copy.61), kind=kOutput, calls=%fused_computation.141 | convolution fusion | flops 12647936 | bytes 1443840 | tf_op jit(solution)/shard_map/ikc,jkc->ijc/dot_general | solution.py:65
  60.5 1.3 fusion.3
  61.8 1.8 %fusion.49 = f32[32,16,128]{2,1,0:T(8,128)} fusion(f32[32,16,128]{2,1,0:T(8,128)S(1)} %fusion.3, bf16[32,16,128]{2,1,0:T(8,128)(2,1)} %param.15, bf16[128,128]{1,0:T(8,128)(2,1)} %param.19), kind=kOutput, calls=%fused_computation.71 | convolution fusion | flops 16973824 | bytes 688128 | tf_op jit(solution)/shard_map/dot_general | solution.py:79
  63.6 2.4 %copy.63 = f32[32,16,128]{0,1,2:T(8,128)} copy(f32[32,16,128]{2,1,0:T(8,128)} %fusion.49) | data formatting | bytes 524288 | tf_op jit(solution)/shard_map/dot_general | solution.py:79
  66.0 1.9 %multiply_reduce_fusion.2 = (f32[32,16]{0,1:T(8,128)S(1)}, f32[32,16]{0,1:T(8,128)S(1)}) fusion(f32[32,16,128]{0,1,2:T(8,128)} %copy.63, f32[128]{0:T(128)} %param.22, f32[32,16]{0,1:T(8,128)} %add_rsqrt_fusion.1, f32[32,16,128]{0,1,2:T(8,128)} %copy-done.1, f32[32,16]{0,1:T(8,128)} %copy-done.15), kind=kLoop, calls=%fused_computation.15 | loop fusion | flops 392192 | bytes 532992 | tf_op jit(solution)/shard_map/reduce_sum | solution.py:20
  67.9 2.8 %multiply_convert_fusion = (bf16[32,16,128]{0,1,2:T(8,128)(2,1)S(1)}, bf16[32,16,128]{0,1,2:T(8,128)(2,1)}) fusion(f32[32,16,128]{0,1,2:T(8,128)} %copy.63, f32[32,16,128]{0,1,2:T(8,128)} %copy-done.1, f32[32,16]{0,1:T(8,128)S(1)} %get-tuple-element.25, f32[32,16]{0,1:T(8,128)S(1)} %get-tuple-element.26, f32[128]{0:T(128)} %param.22, ...), kind=kLoop, calls=%fused_computation.10 | loop fusion | flops 720896 | bytes 795648 | tf_op jit(solution)/shard_map/convert_element_type | solution.py:80
  71.5 2.6 %fusion.101 = bf16[128,96,16]{1,2,0:T(8,128)(2,1)} fusion(bf16[32,96,128]{0,1,2:T(8,128)(2,1)S(1)} %copy.61, bf16[32,16,128]{0,1,2:T(8,128)(2,1)S(1)} %get-tuple-element.14), kind=kOutput, calls=%fused_computation.142 | convolution fusion | flops 12582912 | bytes 1310720 | tf_op jit(solution)/shard_map/ijc,ikc->kjc/dot_general | solution.py:93
  74.1 2.5 %copy.67 = bf16[128,96,16]{0,2,1:T(8,128)(2,1)} copy(bf16[128,96,16]{1,2,0:T(8,128)(2,1)} %fusion.101) | data formatting | bytes 786432 | tf_op jit(solution)/shard_map/ijc,ikc->kjc/dot_general | solution.py:93
  76.9 1.7 %fusion = bf16[96,32,128]{0,1,2:T(8,128)(2,1)S(1)} fusion(bf16[16,96,128]{1,0,2:T(8,128)(2,1)} %copy.60, bf16[32,16,128]{0,1,2:T(8,128)(2,1)} %copy-done.4), kind=kOutput, calls=%fused_computation.1 | convolution fusion | flops 12976128 | bytes 1310720 | tf_op jit(solution)/shard_map/ijc,jkc->kic/dot_general | solution.py:84
  78.6 1.7 %copy.65 = bf16[96,32,128]{2,0,1:T(8,128)(2,1)} copy(bf16[96,32,128]{0,1,2:T(8,128)(2,1)S(1)} %fusion) | data formatting | bytes 1572864 | tf_op jit(solution)/shard_map/convert_element_type | solution.py:86
  80.9 1.6 %multiply_convert_fusion.2 = (bf16[32,16,128]{2,1,0:T(8,128)(2,1)}, f32[32,16,128]{2,1,0:T(8,128)S(1)}) fusion(f32[32,16,128]{2,1,0:T(8,128)S(1)} %fusion.3, bf16[32,16,128]{2,1,0:T(8,128)(2,1)S(1)} %copy.62, bf16[128,128]{1,0:T(8,128)(2,1)} %param.19), kind=kOutput, calls=%fused_computation.65 | convolution fusion | flops 16908288 | bytes 819200 | tf_op jit(solution)/shard_map/dot_general | solution.py:69
  82.5 1.3 fusion.98
  85.4 1.0 fusion.36
  86.4 20.3 %reduce-scatter.3.cloned.1.call-done = bf16[12,16,128]{2,1,0:T(8,128)(2,1)} async-done(((bf16[96,16,128]{2,1,0:T(8,128)(2,1)}), bf16[12,16,128]{2,1,0:T(8,128)(2,1)}) %reduce-scatter.3.cloned.1.call-update) | async-done | bytes 49168 | tf_op jit(solution)/shard_map/reduce_scatter | solution.py:92
  107.9 20.2 %all-reduce.3.cloned.1.call-done = bf16[96,32,128]{2,0,1:T(8,128)(2,1)} async-done(((bf16[96,32,128]{2,0,1:T(8,128)(2,1)}), bf16[96,32,128]{2,0,1:T(8,128)(2,1)}) %all-reduce.3.cloned.1.call-update) | async-done | bytes 786448
  128.0 1.1 fusion.22
  130.5 1.2 fusion.14
  (95 shorter events, 10.8 us)
Async XLA Ops:
  8.0 3.0 %copy-start = (bf16[128,256]{1,0:T(8,128)(2,1)S(1)}, bf16[128,256]{1,0:T(8,128)(2,1)}, u32[]{:S(2)}) copy-start(bf16[128,256]{1,0:T(8,128)(2,1)} %param.16) | copy-start | bytes 196612
  8.0 98.6 %reduce-scatter.3.cloned.1.call-start = ((), (), s32[]{:S(2)}) async-start(), calls=%async_computation.1 | async-start | bytes 442368 | tf_op jit(solution)/shard_map/reduce_scatter | solution.py:92
  12.4 23.5 %copy-start.11 = (bf16[16,12,128]{2,0,1:T(8,128)(2,1)S(1)}, bf16[16,12,128]{2,0,1:T(8,128)(2,1)}, u32[]{:S(2)}) copy-start(bf16[16,12,128]{2,0,1:T(8,128)(2,1)} %param.13) | copy-start | bytes 147460
  12.4 23.8 %copy-start.20 = (bf16[128,256]{1,0:T(8,128)(2,1)S(1)}, bf16[128,256]{1,0:T(8,128)(2,1)}, u32[]{:S(2)}) copy-start(bf16[128,256]{1,0:T(8,128)(2,1)} %param.17) | copy-start | bytes 196612
  12.4 23.8 %copy-start.22 = (f32[128]{0:T(128)S(1)}, f32[128]{0:T(128)}, u32[]{:S(2)}) copy-start(f32[128]{0:T(128)} %param.20) | copy-start | bytes 1540
  12.4 23.8 %copy-start.25 = (f32[128]{0:T(128)S(1)}, f32[128]{0:T(128)}, u32[]{:S(2)}) copy-start(f32[128]{0:T(128)} %param.21) | copy-start | bytes 1540
  36.0 21.4 %copy-start.16 = (f32[16,12]{0,1:T(8,128)}, f32[16,12]{0,1:T(8,128)S(1)}, u32[]{:S(2)}) copy-start(f32[16,12]{0,1:T(8,128)S(1)} %broadcast_multiply_fusion.5) | copy-start | bytes 2308
  36.2 21.2 %copy-start.18 = (f32[16,12]{0,1:T(8,128)}, f32[16,12]{0,1:T(8,128)S(1)}, u32[]{:S(2)}) copy-start(f32[16,12]{0,1:T(8,128)S(1)} %add_rsqrt_fusion.2) | copy-start | bytes 2308
  53.0 6.2 %copy-start.7 = (bf16[32,16,128]{2,1,0:T(8,128)(2,1)S(1)}, bf16[32,16,128]{2,1,0:T(8,128)(2,1)}, u32[]{:S(2)}) copy-start(bf16[32,16,128]{2,1,0:T(8,128)(2,1)} %param.14) | copy-start | bytes 393220
  57.4 2.0 %copy-start.15 = (f32[32,16]{0,1:T(8,128)}, f32[32,16]{0,1:T(8,128)S(1)}, u32[]{:S(2)}) copy-start(f32[32,16]{0,1:T(8,128)S(1)} %broadcast_multiply_fusion.10) | copy-start | bytes 6148
  74.1 6.3 %copy-start.6 = (bf16[32,16,128]{0,1,2:T(8,128)(2,1)S(1)}, bf16[32,16,128]{0,1,2:T(8,128)(2,1)}, u32[]{:S(2)}) copy-start(bf16[32,16,128]{0,1,2:T(8,128)(2,1)} %get-tuple-element.15) | copy-start | bytes 393220
  76.6 5.9 %copy-start.8 = (bf16[32,16,128]{2,1,0:T(8,128)(2,1)S(1)}, bf16[32,16,128]{2,1,0:T(8,128)(2,1)}, u32[]{:S(2)}) copy-start(bf16[32,16,128]{2,1,0:T(8,128)(2,1)} %param.14) | copy-start | bytes 393220
  76.6 5.9 %copy-start.12 = (f32[32,16]{1,0:T(8,128)S(1)}, f32[32,16]{1,0:T(8,128)}, u32[]{:S(2)}) copy-start(f32[32,16]{1,0:T(8,128)} %copy.59) | copy-start | bytes 6148
  76.6 5.9 %copy-start.23 = (f32[128]{0:T(128)S(1)}, f32[128]{0:T(128)}, u32[]{:S(2)}) copy-start(f32[128]{0:T(128)} %param.20) | copy-start | bytes 1540
  76.6 51.4 %all-reduce.3.cloned.1.call-start = ((), (), s32[]{:S(2)}) async-start(), calls=%async_computation.2 | async-start | bytes 1572864
  78.6 28.1 %copy-start.10 = (f32[16,12,256]{2,0,1:T(8,128)S(1)}, f32[16,12,256]{2,0,1:T(8,128)}, u32[]{:S(2)}) copy-start(f32[16,12,256]{2,0,1:T(8,128)} %copy-done.9) | copy-start | bytes 589828
  78.6 28.9 %copy-start.17 = (f32[16,12]{0,1:T(8,128)S(1)}, f32[16,12]{0,1:T(8,128)}, u32[]{:S(2)}) copy-start(f32[16,12]{0,1:T(8,128)} %copy-done.16) | copy-start | bytes 2308
  78.6 49.4 %copy-start.3 = (f32[32,24,256]{2,1,0:T(8,128)S(1)}, f32[32,24,256]{2,1,0:T(8,128)}, u32[]{:S(2)}) copy-start(f32[32,24,256]{2,1,0:T(8,128)} %copy-done.2) | copy-start | bytes 2359300
  80.3 3.8 %copy-start.26 = (u32[32]{0:T(128)S(1)}, u32[32]{0:T(128)}, u32[]{:S(2)}) copy-start(u32[32]{0:T(128)} %constant.33) | copy-start | bytes 388
  80.3 27.2 %copy-start.19 = (f32[16,12]{0,1:T(8,128)S(1)}, f32[16,12]{0,1:T(8,128)}, u32[]{:S(2)}) copy-start(f32[16,12]{0,1:T(8,128)} %copy-done.18) | copy-start | bytes 2308
  80.3 27.2 %copy-start.21 = (bf16[128,256]{1,0:T(8,128)(2,1)S(1)}, bf16[128,256]{1,0:T(8,128)(2,1)}, u32[]{:S(2)}) copy-start(bf16[128,256]{1,0:T(8,128)(2,1)} %param.17) | copy-start | bytes 196612
  80.3 27.2 %copy-start.24 = (f32[128]{0:T(128)S(1)}, f32[128]{0:T(128)}, u32[]{:S(2)}) copy-start(f32[128]{0:T(128)} %param.20) | copy-start | bytes 1540
  80.3 48.8 %copy-start.5 = (bf16[32,24,128]{2,1,0:T(8,128)(2,1)S(1)}, bf16[32,24,128]{2,1,0:T(8,128)(2,1)}, u32[]{:S(2)}) copy-start(bf16[32,24,128]{2,1,0:T(8,128)(2,1)} %param.12) | copy-start | bytes 589828
  80.3 48.8 %copy-start.14 = (f32[32,24]{1,0:T(8,128)S(1)}, f32[32,24]{1,0:T(8,128)}, u32[]{:S(2)}) copy-start(f32[32,24]{1,0:T(8,128)} %copy-done.13) | copy-start | bytes 9220
  (5 other events, 4.0 us)
Sparse Core Ops, SparseCore 0:
  76.7 29.9 reduce-scatter.2
Sparse Core Ops, SparseCore 1:
  80.5 47.5 all-reduce.2
where the time goes:
time: 140 us; the launch traced here: 139 us
  waiting for transfers between devices  40.5 us (29%)
  blocking collectives  32.1 us (23%)
  local copies, waits for them, and re-layouts  21.4 us (15%)
  between operations  16.6 us (12%)
  matrix products  14.7 us (10%)
  other arithmetic  13.6 us (10%)
    reduce_scatter x1, waiting for transfers between devices, shards(): lax.psum_scatter(jnp.einsum('ijc,ikc->kjc', grad_tri, left_slice, preferr...  20.3 us
    unnamed x3, waiting for transfers between devices  20.2 us
    all_gather x1, blocking collectives, shards(): left_whole = lax.all_gather(left, 'ja', axis=1, tiled=True)  16.3 us
    all_gather x1, blocking collectives, shards(): panel_piece = lax.all_gather(right, 'ia', axis=1, tiled=True)  15.8 us
    all_gather x1, local copies, waits for them, and re-layouts, shards(): left_whole = lax.all_gather(left, 'ja', axis=1, tiled=True)  6.21 us
    unnamed x55, local copies, waits for them, and re-layouts  4.42 us
    convert_element_type x1, other arithmetic, shards(): norm_back(tri_scaled, tri_inverse, grad_tnorm, update_gain)  2.81 us
  transfers between devices with their start and end apart: 2, of which 2 were waited for; matrix products, arithmetic and copies ran while one was open for 7% of the time, Pallas kernels for 0%

commit v1 on v0

v1 whole, which is shorter than its diff:
```python
import functools
import math

import jax
import jax.numpy as jnp
from jax import lax
from jax.experimental import pallas as pl
from jax.experimental.pallas import tpu as pltpu
from jax.sharding import PartitionSpec as P

EPSILON = 1e-05
MESH = pl.DeviceIdType.MESH
F32 = jnp.float32
BF16 = jnp.bfloat16


def chunk_of(count, rows, most):
    return max(d for d in range(1, count + 1) if count % d == 0 and (d * rows <= most or d == 1))


def normalize(values):
    centre = jnp.mean(values, axis=-1, keepdims=True)
    shifted = values - centre
    inverse = lax.rsqrt(jnp.mean(shifted * shifted, axis=-1, keepdims=True) + EPSILON)
    return shifted * inverse, inverse


def norm_back(scaled, inverse, grad_out, gain):
    grad_hat = grad_out * gain
    first_mean = jnp.mean(grad_hat, axis=-1, keepdims=True)
    second_mean = jnp.mean(grad_hat * scaled, axis=-1, keepdims=True)
    return inverse * (grad_hat - first_mean - scaled * second_mean)


def dot(a, b):
    return jnp.dot(a, b, preferred_element_type=F32)


def dot_t(a, b):
    return lax.dot_general(a, b, (((1,), (1,)), ((), ())), preferred_element_type=F32)


def kernel(
    n_ia,
    n_ja,
    slab_ref,
    cols_ref,
    tile_ref,
    cot_ref,
    wl_ref,
    wr_ref,
    wg_ref,
    wo_ref,
    gain_ref,
    bias_ref,
    ugain_ref,
    ubias_ref,
    update_ref,
    gslab_ref,
    gcols_ref,
    gtile_ref,
    xs_l,
    xs_r,
    save_l,
    save_r,
    left_all,
    right_all,
    left_f,
    right_f,
    dl_recv,
    dr_recv,
    tri_t,
    dtri,
    save_t,
    lsend,
    lrecv,
    rsend,
    rrecv,
    dlsend,
    dlrecv,
    drsend,
    drrecv,
):
    my_ia, my_ja = lax.axis_index("ia"), lax.axis_index("ja")
    rows_i, k_l, ch = slab_ref.shape
    rows_j, k_r, _ = cols_ref.shape
    res = k_l * n_ja

    def ja_peer(s):
        return lax.rem(my_ja + s, n_ja)

    def ia_peer(s):
        return lax.rem(my_ia + s, n_ia)

    barrier = pltpu.get_barrier_semaphore()

    def greet_ja(s, c):
        pl.semaphore_signal(barrier, inc=1, device_id=(my_ia, ja_peer(s)), device_id_type=MESH)
        return c

    def greet_ia(s, c):
        pl.semaphore_signal(barrier, inc=1, device_id=(ia_peer(s), my_ja), device_id_type=MESH)
        return c

    lax.fori_loop(1, n_ja, greet_ja, 0)
    lax.fori_loop(1, n_ia, greet_ia, 0)

    gain = gain_ref[...]
    bias = bias_ref[...]
    ugain = ugain_ref[...]
    ubias = ubias_ref[...]

    def project(x_ref, xs, w_ref, save, edges, base):
        rows, count, _ = x_ref.shape
        pitch = xs.shape[0] // rows

        def widen(r, c):
            xs[pl.ds(pl.multiple_of(r * pitch, 8), count), :] = x_ref[r].astype(F32)
            return c

        lax.fori_loop(0, rows, widen, 0, unroll=4)
        step = chunk_of(count, rows, 256)

        def body(t, c):
            k0 = t * step
            x = jnp.concatenate(
                [xs[pl.ds(k0 + u, rows, stride=pitch), :] for u in range(step)], axis=0
            )
            scaled, inverse = normalize(x)
            q = dot((scaled * gain + bias).astype(BF16), w_ref[...])
            linear = q[:, :ch]
            sigma = jax.nn.sigmoid(q[:, ch:])
            at = pl.ds(pl.multiple_of(k0 * rows, 8), step * rows)
            save[0, at, :] = scaled
            save[1, at, :] = jnp.broadcast_to(inverse, scaled.shape)
            save[2, at, :] = linear
            save[3, at, :] = sigma
            edge = (sigma * linear).astype(BF16)
            edges[pl.ds(base + k0, step)] = edge.reshape(step, rows, ch)
            return c

        lax.fori_loop(0, count // step, body, 0)

    def left_copy(s):
        own = left_all.at[pl.ds(my_ja * k_l, k_l)]
        return pltpu.make_async_remote_copy(
            src_ref=own,
            dst_ref=own,
            send_sem=lsend.at[s],
            recv_sem=lrecv.at[s],
            device_id=(my_ia, ja_peer(s)),
            device_id_type=MESH,
        )

    def right_copy(s):
        own = right_all.at[pl.ds(my_ia * k_r, k_r)]
        return pltpu.make_async_remote_copy(
            src_ref=own,
            dst_ref=own,
            send_sem=rsend.at[s],
            recv_sem=rrecv.at[s],
            device_id=(ia_peer(s), my_ja),
            device_id_type=MESH,
        )

    def dl_copy(s):
        to = ja_peer(s)
        return pltpu.make_async_remote_copy(
            src_ref=left_all.at[pl.ds(to * k_l, k_l)],
            dst_ref=dl_recv.at[s],
            send_sem=dlsend.at[s],
            recv_sem=dlrecv.at[s],
            device_id=(my_ia, to),
            device_id_type=MESH,
        )

    def dr_copy(s):
        to = ia_peer(s)
        return pltpu.make_async_remote_copy(
            src_ref=right_all.at[pl.ds(to * k_r, k_r)],
            dst_ref=dr_recv.at[s],
            send_sem=drsend.at[s],
            recv_sem=drrecv.at[s],
            device_id=(to, my_ja),
            device_id_type=MESH,
        )

    def each(copy, n, act):
        def body(s, c):
            act(copy(s))
            return c

        lax.fori_loop(1, n, body, 0)

    project(cols_ref, xs_r, wr_ref, save_r, right_all, my_ia * k_r)
    pl.semaphore_wait(barrier, n_ia + n_ja - 2)
    each(right_copy, n_ia, lambda c: c.start())
    project(slab_ref, xs_l, wl_ref, save_l, left_all, my_ja * k_l)
    each(left_copy, n_ja, lambda c: c.start())

    t_rows = chunk_of(rows_i, rows_j, 128)
    t_flat = t_rows * rows_j

    def tile_slot(t):
        return pl.ds(pl.multiple_of(t * t_flat, 8), t_flat)

    def gate_body(t, c):
        x = tile_ref[pl.ds(t * t_rows, t_rows)].astype(F32).reshape(t_flat, ch)
        scaled, inverse = normalize(x)
        gate = jax.nn.sigmoid(dot((scaled * gain + bias).astype(BF16), wg_ref[...]))
        at = tile_slot(t)
        save_t[0, at, :] = scaled
        save_t[1, at, :] = jnp.broadcast_to(inverse, scaled.shape)
        save_t[2, at, :] = gate
        return c

    lax.fori_loop(0, rows_i // t_rows, gate_body, 0)

    each(right_copy, n_ia, lambda c: c.wait())
    each(left_copy, n_ja, lambda c: c.wait())

    def to_f32(k, c):
        left_f[k] = left_all[k].astype(F32)
        right_f[k] = right_all[k].astype(F32)
        return c

    lax.fori_loop(0, res, to_f32, 0, unroll=4)

    block = math.gcd(rows_j, 8)
    for first in range(0, rows_j, block):

        def tri_body(k, accs, first=first):
            l = left_f[k]
            return tuple(
                acc + right_f[k, pl.ds(first + j, 1), :] * l for j, acc in enumerate(accs)
            )

        accs = lax.fori_loop(
            0, res, tri_body, tuple(jnp.zeros((rows_i, ch), F32) for _ in range(block)), unroll=2
        )
        for j, acc in enumerate(accs):
            tri_t[pl.ds((first + j) * rows_i, rows_i), :] = acc

    def tile_body(t, c):
        at = tile_slot(t)
        tri = jnp.concatenate(
            [tri_t[pl.ds(t * t_rows + u, rows_j, stride=rows_i), :] for u in range(t_rows)], axis=0
        )
        scaled, inverse = normalize(tri)
        outer = dot((scaled * ugain + ubias).astype(BF16), wo_ref[...])
        gate = save_t[2, at, :]
        update_ref[pl.ds(t * t_rows, t_rows)] = (
            (gate * outer).astype(BF16).reshape(t_rows, rows_j, ch)
        )
        cot = cot_ref[pl.ds(t * t_rows, t_rows)].astype(F32).reshape(t_flat, ch)
        d_outer = (cot * gate).astype(BF16)
        save_t[3, at, :] = cot * outer * gate * (1.0 - gate)
        d_tri = norm_back(scaled, inverse, dot_t(d_outer, wo_ref[...]), ugain)
        d_tri = d_tri.astype(BF16).astype(F32)
        dtri[at, :] = d_tri
        for u in range(t_rows):
            tri_t[pl.ds(t * t_rows + u, rows_j, stride=rows_i), :] = d_tri[
                u * rows_j : (u + 1) * rows_j
            ]
        return c

    lax.fori_loop(0, rows_i // t_rows, tile_body, 0)

    def left_part(s):
        k_first = ja_peer(s) * k_l
        u_l = math.gcd(k_l, 4)

        def body(t, c):
            k0 = k_first + t * u_l
            accs = [None] * u_l
            for j in range(rows_j):
                d = tri_t[pl.ds(j * rows_i, rows_i), :]
                for u in range(u_l):
                    term = right_f[k0 + u, pl.ds(j, 1), :] * d
                    accs[u] = term if j == 0 else accs[u] + term
            for u in range(u_l):
                left_all[k0 + u] = accs[u].astype(BF16)
            return c

        lax.fori_loop(0, k_l // u_l, body, 0)

    def right_part(s):
        k_first = ia_peer(s) * k_r
        u_r = math.gcd(k_r, 4)

        def body(t, c):
            k0 = k_first + t * u_r
            accs = [None] * u_r
            for i in range(rows_i):
                d = dtri[pl.ds(i * rows_j, rows_j), :]
                for u in range(u_r):
                    term = left_f[k0 + u, pl.ds(i, 1), :] * d
                    accs[u] = term if i == 0 else accs[u] + term
            for u in range(u_r):
                right_all[k0 + u] = accs[u].astype(BF16)
            return c

        lax.fori_loop(0, k_r // u_r, body, 0)

    groups = min(n_ia, n_ja)

    def group_body(g, c):
        def one_right(v, c):
            s = g * (n_ia // groups) + v + 1
            right_part(s)

            @pl.when(s < n_ia)
            def _():
                dr_copy(s).start()

            return c

        def one_left(v, c):
            s = g * (n_ja // groups) + v + 1
            left_part(s)

            @pl.when(s < n_ja)
            def _():
                dl_copy(s).start()

            return c

        lax.fori_loop(0, n_ia // groups, one_right, 0)
        lax.fori_loop(0, n_ja // groups, one_left, 0)
        return c

    lax.fori_loop(0, groups, group_body, 0)

    def tile_back(t, c):
        at = tile_slot(t)
        grad = dot_t(save_t[3, at, :].astype(BF16), wg_ref[...])
        out = norm_back(save_t[0, at, :], save_t[1, at, :], grad, gain)
        gtile_ref[pl.ds(t * t_rows, t_rows)] = out.astype(BF16).reshape(t_rows, rows_j, ch)
        return c

    lax.fori_loop(0, rows_i // t_rows, tile_back, 0)

    def project_back(out_ref, xs, w_ref, save, edges, base, recv, n):
        rows, count, _ = out_ref.shape
        pitch = xs.shape[0] // rows
        step = chunk_of(count, rows, 256)

        def body(t, c):
            k0 = t * step
            at = pl.ds(pl.multiple_of(k0 * rows, 8), step * rows)
            d = edges[pl.ds(base + k0, step)].astype(F32)

            def add(s, d):
                return d + recv[s, pl.ds(k0, step)].astype(F32)

            d = lax.fori_loop(1, n, add, d, unroll=n <= 8).reshape(step * rows, ch)
            linear, sigma = save[2, at, :], save[3, at, :]
            p = jnp.concatenate([d * sigma, d * linear * sigma * (1.0 - sigma)], axis=-1)
            grad = dot_t(p.astype(BF16), w_ref[...])
            out = norm_back(save[0, at, :], save[1, at, :], grad, gain)
            for u in range(step):
                xs[pl.ds(k0 + u, rows, stride=pitch), :] = out[u * rows : (u + 1) * rows]
            return c

        lax.fori_loop(0, count // step, body, 0)

        def narrow(r, c):
            out_ref[r] = xs[pl.ds(pl.multiple_of(r * pitch, 8), count), :].astype(BF16)
            return c

        lax.fori_loop(0, rows, narrow, 0, unroll=4)

    each(dr_copy, n_ia, lambda c: c.wait())
    project_back(gcols_ref, xs_r, wr_ref, save_r, right_all, my_ia * k_r, dr_recv, n_ia)
    each(dl_copy, n_ja, lambda c: c.wait())
    project_back(gslab_ref, xs_l, wl_ref, save_l, left_all, my_ja * k_l, dl_recv, n_ja)


def solution(mesh):
    n_ia, n_ja = mesh.shape["ia"], mesh.shape["ja"]

    def shards(slab, cols, tile, cot, wl, wr, wg, wo, gain, bias, ugain, ubias):
        rows_i, k_l, ch = slab.shape
        rows_j, k_r, _ = cols.shape
        res = k_l * n_ja
        pad_l, pad_r = -(-k_l // 8) * 8, -(-k_r // 8) * 8
        vmem = pl.BlockSpec(memory_space=pltpu.VMEM)
        flat = rows_i * rows_j
        dma = pltpu.SemaphoreType.DMA
        return pl.pallas_call(
            functools.partial(kernel, n_ia, n_ja),
            out_shape=[jax.ShapeDtypeStruct(a.shape, BF16) for a in (tile, slab, cols, tile)],
            in_specs=[vmem] * 12,
            out_specs=[vmem] * 4,
            scratch_shapes=[
                pltpu.VMEM((rows_i * pad_l, ch), F32),
                pltpu.VMEM((rows_j * pad_r, ch), F32),
                pltpu.VMEM((4, rows_i * k_l, ch), F32),
                pltpu.VMEM((4, rows_j * k_r, ch), F32),
                pltpu.VMEM((res, rows_i, ch), BF16),
                pltpu.VMEM((res, rows_j, ch), BF16),
                pltpu.VMEM((res, rows_i, ch), F32),
                pltpu.VMEM((res, rows_j, ch), F32),
                pltpu.VMEM((n_ja, k_l, rows_i, ch), BF16),
                pltpu.VMEM((n_ia, k_r, rows_j, ch), BF16),
                pltpu.VMEM((flat, ch), F32),
                pltpu.VMEM((flat, ch), F32),
                pltpu.VMEM((4, flat, ch), F32),
            ]
            + [dma((n,)) for n in (n_ja, n_ja, n_ia, n_ia, n_ja, n_ja, n_ia, n_ia)],
            compiler_params=pltpu.CompilerParams(
                collective_id=0, has_side_effects=True, vmem_limit_bytes=56 * 1024 * 1024
            ),
        )(
            slab, cols, tile, cot, wl, wr, wg, wo,
            gain[None, :], bias[None, :], ugain[None, :], ubias[None, :],
        )

    return jax.shard_map(
        shards,
        mesh=mesh,
        in_specs=(
            P("ia", "ja", None),
            P("ja", "ia", None),
            P("ia", "ja", None),
            P("ia", "ja", None),
        )
        + (P(),) * 8,
        out_specs=(
            P("ia", "ja", None),
            P("ia", "ja", None),
            P("ja", "ia", None),
            P("ia", "ja", None),
        ),
        check_vma=False,
    )
```

time: 140 us -> 43.1 us (0.31)
  waiting for transfers between devices: 40.5 us -> 0 us
  Pallas kernels: 0 us -> 36 us
  blocking collectives: 32.1 us -> 0 us
  between operations: 16.6 us -> 0.65 us
  local copies, waits for them, and re-layouts: 21.4 us -> 6.16 us
  matrix products: 14.7 us -> 0 us
  other arithmetic: 13.6 us -> 0 us
    pallas_call x0 -> x1, Pallas kernels: none -> 36 us  [shards(): pl.pallas_call(functools.partial(kernel, n_ia, n_ja), out_shape=[jax.Shap...]
    all_gather x2 -> x0, blocking collectives: 32.1 us -> none  [the longest x1 16.3 us: shards(): left_whole = lax.all_gather(left, 'ja', axis=1, tiled=True)]
    reduce_scatter x1 -> x0, waiting for transfers between devices: 20.3 us -> none  [shards(): lax.psum_scatter(jnp.einsum('ijc,ikc->kjc', grad_tri, left_slice, preferr...]
    unnamed x3 -> x0, waiting for transfers between devices: 20.2 us -> none
    dot_general x11 -> x0, matrix products: 14.7 us -> none  [the longest x1 2.58 us: shards(): jnp.einsum('ijc,ikc->kjc', grad_tri, left_slice, preferred_element_type=j...]
    all_gather x2 -> x0, local copies, waits for them, and re-layouts: 8.65 us -> none  [the longest x1 6.21 us: shards(): left_whole = lax.all_gather(left, 'ja', axis=1, tiled=True)]
    convert_element_type x6 -> x0, other arithmetic: 5.91 us -> none  [the longest x1 2.81 us: shards(): norm_back(tri_scaled, tri_inverse, grad_tnorm, update_gain)]
    reduce_sum x8 -> x0, other arithmetic: 5.06 us -> none  [the longest x1 1.88 us: norm_back(): first_mean = jnp.mean(grad_hat, axis=-1, keepdims=True)]
  transfers between devices with their start and end apart: 2 -> 0, of which waited for: 2 -> 0; matrix products, arithmetic and copies ran while one was open for 7% -> 0% of each run, Pallas kernels for 0% -> 0%
where the time goes in v1:
time: 43.1 us; the launch traced here: 42.8 us
  Pallas kernels  36 us (84%)
  local copies, waits for them, and re-layouts  6.16 us (14%)
  between operations  0.65 us (2%)
    pallas_call x1, Pallas kernels, shards(): pl.pallas_call(functools.partial(kernel, n_ia, n_ja), out_shape=[jax.Shap...  36 us
    unnamed x8, local copies, waits for them, and re-layouts  4.64 us
    pallas_call x1, local copies, waits for them, and re-layouts, shards(): pl.pallas_call(functools.partial(kernel, n_ia, n_ja), out_shape=[jax.Shap...  1.51 us

profile of v1, /device:TPU:0, one launch (start us, length us, event | category | flops | bytes accessed | tf_op | source)
XLA Modules:
  0.0 42.8 jit_solution(12002263738770469430)
XLA Ops:
  0.6 1.4 %copy.16.cols_ref = bf16[16,12,128]{2,1,0:T(8,128)(2,1)} copy(bf16[16,12,128]{2,0,1:T(8,128)(2,1)} %param.13) | data formatting | bytes 98304 | tf_op args[1]
  2.1 36.0 %shard_map.147 = (bf16[32,16,128]{2,1,0:T(8,128)(2,1)}, bf16[32,24,128]{2,1,0:T(8,128)(2,1)}, bf16[16,12,128]{2,1,0:T(8,128)(2,1)}, bf16[32,16,128]{2,1,0:T(8,128)(2,1)}) custom-call(bf16[32,24,128]{2,1,0:T(8,128)(2,1)} %slab_ref.1, bf16[16,12,128]{2,1,0:T(8,128)(2,1)} %copy.16.cols_ref, bf16[32,16,128]{2,1,0:T(8,128)(2,1)} %tile_ref.1, ...), custom_call_target="tpu_custom_call" | custom-call | tf_op jit(solution)/shard_map/pallas_call | solution.py:390
  38.1 0.0 copy-start
  38.1 1.5 %copy.17 = bf16[16,12,128]{2,0,1:T(8,128)(2,1)} copy(bf16[16,12,128]{2,1,0:T(8,128)(2,1)} %get-tuple-element.6) | data formatting | bytes 98304 | tf_op jit(solution)/shard_map/pallas_call | solution.py:390
  39.6 1.6 %copy.21 = bf16[32,16,128]{2,1,0:T(8,128)(2,1)} copy(bf16[32,16,128]{2,1,0:T(8,128)(2,1)} %get-tuple-element.12) | data formatting | bytes 262144
  41.2 0.0 copy-done
  41.2 0.0 copy-start.1
  41.2 0.7 %copy.22 = bf16[32,24,128]{2,1,0:T(8,128)(2,1)} copy(bf16[32,24,128]{2,1,0:T(8,128)(2,1)S(1)} %copy-done) | data formatting | bytes 393216
  41.9 0.3 copy-done.1
  42.2 0.7 %copy.23 = bf16[32,16,128]{2,1,0:T(8,128)(2,1)} copy(bf16[32,16,128]{2,1,0:T(8,128)(2,1)S(1)} %copy-done.1) | data formatting | bytes 262144
Async XLA Ops:
  38.1 3.1 %copy-start = (bf16[32,24,128]{2,1,0:T(8,128)(2,1)S(1)}, bf16[32,24,128]{2,1,0:T(8,128)(2,1)}, u32[]{:S(2)}) copy-start(bf16[32,24,128]{2,1,0:T(8,128)(2,1)} %get-tuple-element.13) | copy-start | bytes 589828
  41.2 1.0 %copy-start.1 = (bf16[32,16,128]{2,1,0:T(8,128)(2,1)S(1)}, bf16[32,16,128]{2,1,0:T(8,128)(2,1)}, u32[]{:S(2)}) copy-start(bf16[32,16,128]{2,1,0:T(8,128)(2,1)} %get-tuple-element.15) | copy-start | bytes 393220

commit v2 on v1

--- a/solution.py
+++ b/solution.py
@@ -43,6 +43,22 @@
 def kernel(
     n_ia,
     n_ja,
+    slab_hbm,
+    cols_hbm,
+    tile_hbm,
+    cot_hbm,
+    wl_hbm,
+    wr_hbm,
+    wg_hbm,
+    wo_hbm,
+    gain_hbm,
+    bias_hbm,
+    ugain_hbm,
+    ubias_hbm,
+    update_hbm,
+    gslab_hbm,
+    gcols_hbm,
+    gtile_hbm,
     slab_ref,
     cols_ref,
     tile_ref,
@@ -59,8 +75,9 @@
     gslab_ref,
     gcols_ref,
     gtile_ref,
+    in_sem,
+    out_sem,
     xs_l,
-    xs_r,
     save_l,
     save_r,
     left_all,
@@ -83,8 +100,40 @@
 ):
     my_ia, my_ja = lax.axis_index("ia"), lax.axis_index("ja")
     rows_i, k_l, ch = slab_ref.shape
-    rows_j, k_r, _ = cols_ref.shape
-    res = k_l * n_ja
+    k_r, rows_j, _ = cols_ref.shape
+
+    ins = [
+        pltpu.make_async_copy(a, b, in_sem.at[n])
+        for n, (a, b) in enumerate(
+            [
+                (cols_hbm, cols_ref),
+                (wr_hbm, wr_ref),
+                (gain_hbm, gain_ref),
+                (bias_hbm, bias_ref),
+                (slab_hbm, slab_ref),
+                (wl_hbm, wl_ref),
+                (tile_hbm, tile_ref),
+                (wg_hbm, wg_ref),
+                (cot_hbm, cot_ref),
+                (wo_hbm, wo_ref),
+                (ugain_hbm, ugain_ref),
+                (ubias_hbm, ubias_ref),
+            ]
+        )
+    ]
+    outs = [
+        pltpu.make_async_copy(a, b, out_sem.at[n])
+        for n, (a, b) in enumerate(
+            [
+                (update_ref, update_hbm),
+                (gtile_ref, gtile_hbm),
+                (gcols_ref, gcols_hbm),
+                (gslab_ref, gslab_hbm),
+            ]
+        )
+    ]
+    for copy in ins:
+        copy.start()
 
     def ja_peer(s):
         return lax.rem(my_ja + s, n_ja)
@@ -105,27 +154,26 @@
     lax.fori_loop(1, n_ja, greet_ja, 0)
     lax.fori_loop(1, n_ia, greet_ia, 0)
 
+    for copy in ins[:4]:
+        copy.wait()
     gain = gain_ref[...]
     bias = bias_ref[...]
-    ugain = ugain_ref[...]
-    ubias = ubias_ref[...]
-
-    def project(x_ref, xs, w_ref, save, edges, base):
-        rows, count, _ = x_ref.shape
-        pitch = xs.shape[0] // rows
-
-        def widen(r, c):
-            xs[pl.ds(pl.multiple_of(r * pitch, 8), count), :] = x_ref[r].astype(F32)
-            return c
-
-        lax.fori_loop(0, rows, widen, 0, unroll=4)
+    pitch = xs_l.shape[0] // rows_i
+
+    def slab_piece(k0, step):
+        return jnp.concatenate(
+            [xs_l[pl.ds(k0 + u, rows_i, stride=pitch), :] for u in range(step)], axis=0
+        )
+
+    def cols_piece(k0, step):
+        return cols_ref[pl.ds(k0, step)].astype(F32).reshape(step * rows_j, ch)
+
+    def project(piece, rows, count, w_ref, save, edges, base):
         step = chunk_of(count, rows, 256)
 
         def body(t, c):
             k0 = t * step
-            x = jnp.concatenate(
-                [xs[pl.ds(k0 + u, rows, stride=pitch), :] for u in range(step)], axis=0
-            )
+            x = piece(k0, step)
             scaled, inverse = normalize(x)
             q = dot((scaled * gain + bias).astype(BF16), w_ref[...])
             linear = q[:, :ch]
@@ -192,12 +240,24 @@
 
         lax.fori_loop(1, n, body, 0)
 
-    project(cols_ref, xs_r, wr_ref, save_r, right_all, my_ia * k_r)
+    project(cols_piece, rows_j, k_r, wr_ref, save_r, right_all, my_ia * k_r)
     pl.semaphore_wait(barrier, n_ia + n_ja - 2)
     each(right_copy, n_ia, lambda c: c.start())
-    project(slab_ref, xs_l, wl_ref, save_l, left_all, my_ja * k_l)
+    for copy in ins[4:6]:
+        copy.wait()
+
+    def widen(r, c):
+        xs_l[pl.ds(pl.multiple_of(r * pitch, 8), k_l), :] = slab_ref[r].astype(F32)
+        return c
+
+    lax.fori_loop(0, rows_i, widen, 0, unroll=4)
+    project(slab_piece, rows_i, k_l, wl_ref, save_l, left_all, my_ja * k_l)
     each(left_copy, n_ja, lambda c: c.start())
 
+    for copy in ins[6:]:
+        copy.wait()
+    ugain = ugain_ref[...]
+    ubias = ubias_ref[...]
     t_rows = chunk_of(rows_i, rows_j, 128)
     t_flat = t_rows * rows_j
 
@@ -217,29 +277,39 @@
     lax.fori_loop(0, rows_i // t_rows, gate_body, 0)
 
     each(right_copy, n_ia, lambda c: c.wait())
-    each(left_copy, n_ja, lambda c: c.wait())
-
-    def to_f32(k, c):
-        left_f[k] = left_all[k].astype(F32)
-        right_f[k] = right_all[k].astype(F32)
-        return c
-
-    lax.fori_loop(0, res, to_f32, 0, unroll=4)
 
     block = math.gcd(rows_j, 8)
-    for first in range(0, rows_j, block):
-
-        def tri_body(k, accs, first=first):
-            l = left_f[k]
-            return tuple(
-                acc + right_f[k, pl.ds(first + j, 1), :] * l for j, acc in enumerate(accs)
-            )
-
-        accs = lax.fori_loop(
-            0, res, tri_body, tuple(jnp.zeros((rows_i, ch), F32) for _ in range(block)), unroll=2
-        )
-        for j, acc in enumerate(accs):
-            tri_t[pl.ds((first + j) * rows_i, rows_i), :] = acc
+
+    def tri_chunk(s, c):
+        @pl.when(s > 0)
+        def _():
+            left_copy(s).wait()
+
+        k_first = lax.rem(my_ja - s + n_ja, n_ja) * k_l
+
+        def to_f32(k, c):
+            left_f[k] = left_all[k].astype(F32)
+            right_f[k] = right_all[k].astype(F32)
+            return c
+
+        lax.fori_loop(k_first, k_first + k_l, to_f32, 0)
+        for first in range(0, rows_j, block):
+
+            def tri_body(k, accs, first=first):
+                l = left_f[k_first + k]
+                return tuple(
+                    acc + right_f[k_first + k, pl.ds(first + j, 1), :] * l
+                    for j, acc in enumerate(accs)
+                )
+
+            accs = tuple(tri_t[pl.ds((first + j) * rows_i, rows_i), :] for j in range(block))
+            accs = lax.fori_loop(0, k_l, tri_body, accs, unroll=2)
+            for j, acc in enumerate(accs):
+                tri_t[pl.ds((first + j) * rows_i, rows_i), :] = acc
+        return c
+
+    tri_t[...] = jnp.zeros_like(tri_t)
+    lax.fori_loop(0, n_ja, tri_chunk, 0)
 
     def tile_body(t, c):
         at = tile_slot(t)
@@ -265,6 +335,7 @@
         return c
 
     lax.fori_loop(0, rows_i // t_rows, tile_body, 0)
+    outs[0].start()
 
     def left_part(s):
         k_first = ja_peer(s) * k_l
@@ -339,10 +410,9 @@
         return c
 
     lax.fori_loop(0, rows_i // t_rows, tile_back, 0)
-
-    def project_back(out_ref, xs, w_ref, save, edges, base, recv, n):
-        rows, count, _ = out_ref.shape
-        pitch = xs.shape[0] // rows
+    outs[1].start()
+
+    def project_back(put, rows, count, w_ref, save, edges, base, recv, n):
         step = chunk_of(count, rows, 256)
 
         def body(t, c):
@@ -357,64 +427,103 @@
             linear, sigma = save[2, at, :], save[3, at, :]
             p = jnp.concatenate([d * sigma, d * linear * sigma * (1.0 - sigma)], axis=-1)
             grad = dot_t(p.astype(BF16), w_ref[...])
-            out = norm_back(save[0, at, :], save[1, at, :], grad, gain)
-            for u in range(step):
-                xs[pl.ds(k0 + u, rows, stride=pitch), :] = out[u * rows : (u + 1) * rows]
+            put(k0, step, norm_back(save[0, at, :], save[1, at, :], grad, gain))
             return c
 
         lax.fori_loop(0, count // step, body, 0)
 
-        def narrow(r, c):
-            out_ref[r] = xs[pl.ds(pl.multiple_of(r * pitch, 8), count), :].astype(BF16)
-            return c
-
-        lax.fori_loop(0, rows, narrow, 0, unroll=4)
+    def put_cols(k0, step, out):
+        gcols_ref[pl.ds(k0, step)] = out.astype(BF16).reshape(step, rows_j, ch)
+
+    def put_slab(k0, step, out):
+        for u in range(step):
+            xs_l[pl.ds(k0 + u, rows_i, stride=pitch), :] = out[u * rows_i : (u + 1) * rows_i]
 
     each(dr_copy, n_ia, lambda c: c.wait())
-    project_back(gcols_ref, xs_r, wr_ref, save_r, right_all, my_ia * k_r, dr_recv, n_ia)
+    project_back(put_cols, rows_j, k_r, wr_ref, save_r, right_all, my_ia * k_r, dr_recv, n_ia)
+    outs[2].start()
     each(dl_copy, n_ja, lambda c: c.wait())
-    project_back(gslab_ref, xs_l, wl_ref, save_l, left_all, my_ja * k_l, dl_recv, n_ja)
+    project_back(put_slab, rows_i, k_l, wl_ref, save_l, left_all, my_ja * k_l, dl_recv, n_ja)
+
+    def narrow(r, c):
+        gslab_ref[r] = xs_l[pl.ds(pl.multiple_of(r * pitch, 8), k_l), :].astype(BF16)
+        return c
+
+    lax.fori_loop(0, rows_i, narrow, 0, unroll=4)
+    outs[3].start()
+    for copy in outs:
+        copy.wait()
+
+
+def move(*refs):
+    n = len(refs) // 2
+    sem = refs[-1]
+    copies = [pltpu.make_async_copy(refs[m], refs[n + m], sem.at[m]) for m in range(n)]
+    for copy in copies:
+        copy.start()
+    for copy in copies:
+        copy.wait()
 
 
 def solution(mesh):
     n_ia, n_ja = mesh.shape["ia"], mesh.shape["ja"]
 
     def shards(slab, cols, tile, cot, wl, wr, wg, wo, gain, bias, ugain, ubias):
+        cols = jnp.transpose(cols, (1, 0, 2))
         rows_i, k_l, ch = slab.shape
-        rows_j, k_r, _ = cols.shape
+        k_r, rows_j, _ = cols.shape
         res = k_l * n_ja
-        pad_l, pad_r = -(-k_l // 8) * 8, -(-k_r // 8) * 8
-        vmem = pl.BlockSpec(memory_space=pltpu.VMEM)
+        pitch = -(-k_l // 8) * 8
+        anywhere = pl.BlockSpec(memory_space=pl.ANY)
         flat = rows_i * rows_j
         dma = pltpu.SemaphoreType.DMA
-        return pl.pallas_call(
+        ins = (
+            slab, cols, tile, cot, wl, wr, wg, wo,
+            gain[None, :], bias[None, :], ugain[None, :], ubias[None, :],
+        )
+        results = [jax.ShapeDtypeStruct(a.shape, BF16) for a in (tile, slab, cols, tile)]
+        buffers = (
+            [(a.shape, a.dtype) for a in ins]
+            + [(a.shape, a.dtype) for a in results]
+            + [
+                ((rows_i * pitch, ch), F32),
+                ((4, rows_i * k_l, ch), F32),
+                ((4, rows_j * k_r, ch), F32),
+                ((res, rows_i, ch), BF16),
+                ((res, rows_j, ch), BF16),
+                ((res, rows_i, ch), F32),
+                ((res, rows_j, ch), F32),
+                ((n_ja, k_l, rows_i, ch), BF16),
+                ((n_ia, k_r, rows_j, ch), BF16),
+                ((flat, ch), F32),
+                ((flat, ch), F32),
+                ((4, flat, ch), F32),
+            ]
+        )
+        held = sum(math.prod(shape) * jnp.dtype(kind).itemsize for shape, kind in buffers)
+        scratch = [pltpu.VMEM(shape, kind) for shape, kind in buffers]
+        n_io = len(ins) + len(results)
+        done = pl.pallas_call(
             functools.partial(kernel, n_ia, n_ja),
-            out_shape=[jax.ShapeDtypeStruct(a.shape, BF16) for a in (tile, slab, cols, tile)],
-            in_specs=[vmem] * 12,
-            out_specs=[vmem] * 4,
-            scratch_shapes=[
-                pltpu.VMEM((rows_i * pad_l, ch), F32),
-                pltpu.VMEM((rows_j * pad_r, ch), F32),
-                pltpu.VMEM((4, rows_i * k_l, ch), F32),
-                pltpu.VMEM((4, rows_j * k_r, ch), F32),
-                pltpu.VMEM((res, rows_i, ch), BF16),
-                pltpu.VMEM((res, rows_j, ch), BF16),
-                pltpu.VMEM((res, rows_i, ch), F32),
-                pltpu.VMEM((res, rows_j, ch), F32),
-                pltpu.VMEM((n_ja, k_l, rows_i, ch), BF16),
-                pltpu.VMEM((n_ia, k_r, rows_j, ch), BF16),
-                pltpu.VMEM((flat, ch), F32),
-                pltpu.VMEM((flat, ch), F32),
-                pltpu.VMEM((4, flat, ch), F32),
-            ]
+            out_shape=results,
+            in_specs=[pl.BlockSpec(memory_space=pltpu.HBM)] * len(ins),
+            out_specs=[anywhere] * len(results),
+            scratch_shapes=scratch[:n_io]
+            + [dma((len(ins),)), dma((len(results),))]
+            + scratch[n_io:]
             + [dma((n,)) for n in (n_ja, n_ja, n_ia, n_ia, n_ja, n_ja, n_ia, n_ia)],
             compiler_params=pltpu.CompilerParams(
-                collective_id=0, has_side_effects=True, vmem_limit_bytes=56 * 1024 * 1024
+                collective_id=0, has_side_effects=True, vmem_limit_bytes=held + 4 * 1024 * 1024
             ),
-        )(
-            slab, cols, tile, cot, wl, wr, wg, wo,
-            gain[None, :], bias[None, :], ugain[None, :], ubias[None, :],
-        )
+        )(*ins)
+        update, gslab, gcols, gtile = pl.pallas_call(
+            move,
+            out_shape=results,
+            in_specs=[anywhere] * len(results),
+            out_specs=[anywhere] * len(results),
+            scratch_shapes=[dma((len(results),))],
+        )(*done)
+        return update, gslab, jnp.transpose(gcols, (1, 0, 2)), gtile
 
     return jax.shard_map(
         shards,

time: 43.1 us -> 61.3 us (1.42)
  Pallas kernels: 36 us -> 50.2 us
  local copies, waits for them, and re-layouts: 6.16 us -> 9.96 us
    pallas_call x1 -> x2, Pallas kernels: 36 us -> 50.2 us  [the longest x1 33.6 us: shards(): pl.pallas_call(functools.partial(kernel, n_ia, n_ja), out_shape=results,...]
    unnamed x8 -> x32, local copies, waits for them, and re-layouts: 4.64 us -> 9.96 us
    pallas_call x1 -> x0, local copies, waits for them, and re-layouts: 1.51 us -> none  [shards(): pl.pallas_call(functools.partial(kernel, n_ia, n_ja), out_shape=[jax.Shap...]
where the time goes in v2:
time: 61.3 us; the launch traced here: 60.8 us
  Pallas kernels  50.2 us (82%)
  local copies, waits for them, and re-layouts  9.96 us (16%)
  between operations  0.7 us (1%)
    pallas_call x1, Pallas kernels, shards(): pl.pallas_call(functools.partial(kernel, n_ia, n_ja), out_shape=results,...  33.6 us
    pallas_call x1, Pallas kernels, shards(): pl.pallas_call(move, out_shape=results, in_specs=[anywhere] * len(results...  16.5 us
    unnamed x32, local copies, waits for them, and re-layouts  9.96 us

profile of v2, /device:TPU:0, one launch (start us, length us, event | category | flops | bytes accessed | tf_op | source)
XLA Modules:
  0.0 60.8 jit_solution(3582211828168623900)
XLA Ops:
  0.6 0.0 copy-start.15
  0.6 0.0 copy-start.12
  0.7 0.0 copy-start.13
  0.7 0.0 copy-start.14
  0.7 0.6 %copy-done.15 = f32[128]{0:T(128)S(1)} copy-done((f32[128]{0:T(128)S(1)}, f32[128]{0:T(128)}, u32[]{:S(2)}) %copy-start.15) | copy-done | bytes 536
  1.3 0.0 copy-done.12
  1.3 0.0 copy-done.13
  1.3 0.0 copy-done.14
  1.3 0.0 copy-start
  1.3 0.9 %copy-done = bf16[32,24,128]{2,1,0:T(8,128)(2,1)S(1)} copy-done((bf16[32,24,128]{2,1,0:T(8,128)(2,1)S(1)}, bf16[32,24,128]{2,1,0:T(8,128)(2,1)}, u32[]{:S(2)}) %copy-start) | copy-done | bytes 196632
  2.3 0.9 %copy-done.2 = bf16[32,16,128]{2,1,0:T(8,128)(2,1)S(1)} copy-done((bf16[32,16,128]{2,1,0:T(8,128)(2,1)S(1)}, bf16[32,16,128]{2,1,0:T(8,128)(2,1)}, u32[]{:S(2)}) %copy-start.2) | copy-done | bytes 131096
  3.2 0.9 %copy-done.3 = bf16[32,16,128]{2,1,0:T(8,128)(2,1)S(1)} copy-done((bf16[32,16,128]{2,1,0:T(8,128)(2,1)S(1)}, bf16[32,16,128]{2,1,0:T(8,128)(2,1)}, u32[]{:S(2)}) %copy-start.3) | copy-done | bytes 131096
  4.1 0.8 %copy-done.6 = bf16[128,256]{1,0:T(8,128)(2,1)S(1)} copy-done((bf16[128,256]{1,0:T(8,128)(2,1)S(1)}, bf16[128,256]{1,0:T(8,128)(2,1)}, u32[]{:S(2)}) %copy-start.6) | copy-done | bytes 65560
  4.9 0.8 %copy-done.7 = bf16[128,256]{1,0:T(8,128)(2,1)S(1)} copy-done((bf16[128,256]{1,0:T(8,128)(2,1)S(1)}, bf16[128,256]{1,0:T(8,128)(2,1)}, u32[]{:S(2)}) %copy-start.7) | copy-done | bytes 65560
  5.8 0.8 %copy-done.8 = bf16[16,12,128]{2,0,1:T(8,128)(2,1)S(1)} copy-done((bf16[16,12,128]{2,0,1:T(8,128)(2,1)S(1)}, bf16[16,12,128]{2,0,1:T(8,128)(2,1)}, u32[]{:S(2)}) %copy-start.8) | copy-done | bytes 49176
  6.6 0.8 %copy-done.10 = bf16[128,128]{1,0:T(8,128)(2,1)S(1)} copy-done((bf16[128,128]{1,0:T(8,128)(2,1)S(1)}, bf16[128,128]{1,0:T(8,128)(2,1)}, u32[]{:S(2)}) %copy-start.10) | copy-done | bytes 32792
  7.3 0.8 %copy-done.11 = bf16[128,128]{1,0:T(8,128)(2,1)S(1)} copy-done((bf16[128,128]{1,0:T(8,128)(2,1)S(1)}, bf16[128,128]{1,0:T(8,128)(2,1)}, u32[]{:S(2)}) %copy-start.11) | copy-done | bytes 32792
  8.1 33.6 %shard_map.147 = (bf16[32,16,128]{2,1,0:T(8,128)(2,1)S(1)}, bf16[32,24,128]{2,1,0:T(8,128)(2,1)S(1)}, bf16[12,16,128]{2,1,0:T(8,128)(2,1)S(1)}, bf16[32,16,128]{2,1,0:T(8,128)(2,1)S(1)}) custom-call(bf16[32,24,128]{2,1,0:T(8,128)(2,1)S(1)} %copy-done, bf16[12,16,128]{2,1,0:T(8,128)(2,1)S(1)} %bitcast.6, bf16[32,16,128]{2,1,0:T(8,128)(2,1)S(1)} %copy-done.2, ...), custom_call_target="tpu_custom_call" | custom-call | tf_op jit(solution)/shard_map/pallas_call | solution.py:506
  41.7 0.0 copy-start.1
  41.7 0.7 %copy-done.1 = bf16[32,24,128]{2,1,0:T(8,128)(2,1)} copy-done((bf16[32,24,128]{2,1,0:T(8,128)(2,1)}, bf16[32,24,128]{2,1,0:T(8,128)(2,1)S(1)}, u32[]{:S(2)}) %copy-start.1) | copy-done | bytes 196632
  42.4 0.6 %copy-done.4 = bf16[32,16,128]{2,1,0:T(8,128)(2,1)} copy-done((bf16[32,16,128]{2,1,0:T(8,128)(2,1)}, bf16[32,16,128]{2,1,0:T(8,128)(2,1)S(1)}, u32[]{:S(2)}) %copy-start.4) | copy-done | bytes 131096
  43.1 0.6 %copy-done.5 = bf16[32,16,128]{2,1,0:T(8,128)(2,1)} copy-done((bf16[32,16,128]{2,1,0:T(8,128)(2,1)}, bf16[32,16,128]{2,1,0:T(8,128)(2,1)S(1)}, u32[]{:S(2)}) %copy-start.5) | copy-done | bytes 131096
  43.7 0.6 %copy-done.9 = bf16[12,16,128]{2,1,0:T(8,128)(2,1)} copy-done((bf16[12,16,128]{2,1,0:T(8,128)(2,1)}, bf16[12,16,128]{2,1,0:T(8,128)(2,1)S(1)}, u32[]{:S(2)}) %copy-start.9) | copy-done | bytes 49176
  44.3 16.5 %shard_map.148 = (bf16[32,16,128]{2,1,0:T(8,128)(2,1)}, bf16[32,24,128]{2,1,0:T(8,128)(2,1)}, bf16[12,16,128]{2,1,0:T(8,128)(2,1)}, bf16[32,16,128]{2,1,0:T(8,128)(2,1)}) custom-call(bf16[32,16,128]{2,1,0:T(8,128)(2,1)} %copy-done.4, bf16[32,24,128]{2,1,0:T(8,128)(2,1)} %copy-done.1, bf16[12,16,128]{2,1,0:T(8,128)(2,1)} %copy-done.9, ...), custom_call_target="tpu_custom_call" | custom-call | tf_op jit(solution)/shard_map/pallas_call | solution.py:519
  (10 shorter events, 0.0 us)
Async XLA Ops:
  0.6 0.7 %copy-start.15 = (f32[128]{0:T(128)S(1)}, f32[128]{0:T(128)}, u32[]{:S(2)}) copy-start(f32[128]{0:T(128)} %param.23) | copy-start | bytes 1540
  0.6 0.7 %copy-start.12 = (f32[128]{0:T(128)S(1)}, f32[128]{0:T(128)}, u32[]{:S(2)}) copy-start(f32[128]{0:T(128)} %param.20) | copy-start | bytes 1540
  0.7 0.7 %copy-start.13 = (f32[128]{0:T(128)S(1)}, f32[128]{0:T(128)}, u32[]{:S(2)}) copy-start(f32[128]{0:T(128)} %param.21) | copy-start | bytes 1540
  0.7 0.7 %copy-start.14 = (f32[128]{0:T(128)S(1)}, f32[128]{0:T(128)}, u32[]{:S(2)}) copy-start(f32[128]{0:T(128)} %param.22) | copy-start | bytes 1540
  1.3 0.9 %copy-start = (bf16[32,24,128]{2,1,0:T(8,128)(2,1)S(1)}, bf16[32,24,128]{2,1,0:T(8,128)(2,1)}, u32[]{:S(2)}) copy-start(bf16[32,24,128]{2,1,0:T(8,128)(2,1)} %slab_hbm.1) | copy-start | bytes 589828
  2.3 0.9 %copy-start.2 = (bf16[32,16,128]{2,1,0:T(8,128)(2,1)S(1)}, bf16[32,16,128]{2,1,0:T(8,128)(2,1)}, u32[]{:S(2)}) copy-start(bf16[32,16,128]{2,1,0:T(8,128)(2,1)} %tile_hbm.1) | copy-start | bytes 393220
  3.2 0.9 %copy-start.3 = (bf16[32,16,128]{2,1,0:T(8,128)(2,1)S(1)}, bf16[32,16,128]{2,1,0:T(8,128)(2,1)}, u32[]{:S(2)}) copy-start(bf16[32,16,128]{2,1,0:T(8,128)(2,1)} %cot_hbm.1) | copy-start | bytes 393220
  4.1 0.8 %copy-start.6 = (bf16[128,256]{1,0:T(8,128)(2,1)S(1)}, bf16[128,256]{1,0:T(8,128)(2,1)}, u32[]{:S(2)}) copy-start(bf16[128,256]{1,0:T(8,128)(2,1)} %wl_hbm.1) | copy-start | bytes 196612
  4.9 0.8 %copy-start.7 = (bf16[128,256]{1,0:T(8,128)(2,1)S(1)}, bf16[128,256]{1,0:T(8,128)(2,1)}, u32[]{:S(2)}) copy-start(bf16[128,256]{1,0:T(8,128)(2,1)} %wr_hbm.1) | copy-start | bytes 196612
  5.8 0.8 %copy-start.8 = (bf16[16,12,128]{2,0,1:T(8,128)(2,1)S(1)}, bf16[16,12,128]{2,0,1:T(8,128)(2,1)}, u32[]{:S(2)}) copy-start(bf16[16,12,128]{2,0,1:T(8,128)(2,1)} %param.13) | copy-start | bytes 147460
  6.6 0.8 %copy-start.10 = (bf16[128,128]{1,0:T(8,128)(2,1)S(1)}, bf16[128,128]{1,0:T(8,128)(2,1)}, u32[]{:S(2)}) copy-start(bf16[128,128]{1,0:T(8,128)(2,1)} %wg_hbm.1) | copy-start | bytes 98308
  7.3 0.8 %copy-start.11 = (bf16[128,128]{1,0:T(8,128)(2,1)S(1)}, bf16[128,128]{1,0:T(8,128)(2,1)}, u32[]{:S(2)}) copy-start(bf16[128,128]{1,0:T(8,128)(2,1)} %wo_hbm.1) | copy-start | bytes 98308
  41.7 0.7 %copy-start.1 = (bf16[32,24,128]{2,1,0:T(8,128)(2,1)}, bf16[32,24,128]{2,1,0:T(8,128)(2,1)S(1)}, u32[]{:S(2)}) copy-start(bf16[32,24,128]{2,1,0:T(8,128)(2,1)S(1)} %get-tuple-element.13.refs_1_) | copy-start | bytes 589828
  42.4 0.6 %copy-start.4 = (bf16[32,16,128]{2,1,0:T(8,128)(2,1)}, bf16[32,16,128]{2,1,0:T(8,128)(2,1)S(1)}, u32[]{:S(2)}) copy-start(bf16[32,16,128]{2,1,0:T(8,128)(2,1)S(1)} %get-tuple-element.12.refs_0_) | copy-start | bytes 393220
  43.1 0.6 %copy-start.5 = (bf16[32,16,128]{2,1,0:T(8,128)(2,1)}, bf16[32,16,128]{2,1,0:T(8,128)(2,1)S(1)}, u32[]{:S(2)}) copy-start(bf16[32,16,128]{2,1,0:T(8,128)(2,1)S(1)} %get-tuple-element.15.refs_3_) | copy-start | bytes 393220
  43.7 0.6 %copy-start.9 = (bf16[12,16,128]{2,1,0:T(8,128)(2,1)}, bf16[12,16,128]{2,1,0:T(8,128)(2,1)S(1)}, u32[]{:S(2)}) copy-start(bf16[12,16,128]{2,1,0:T(8,128)(2,1)S(1)} %get-tuple-element.14.refs_2_) | copy-start | bytes 147460

commit v3 on v2

--- a/solution.py
+++ b/solution.py
@@ -9,6 +9,7 @@
 from jax.sharding import PartitionSpec as P
 
 EPSILON = 1e-05
+VMEM_BYTES = 56 * 1024 * 1024
 MESH = pl.DeviceIdType.MESH
 F32 = jnp.float32
 BF16 = jnp.bfloat16
@@ -456,12 +457,16 @@
 
 
 def move(*refs):
-    n = len(refs) // 2
-    sem = refs[-1]
-    copies = [pltpu.make_async_copy(refs[m], refs[n + m], sem.at[m]) for m in range(n)]
-    for copy in copies:
+    n = (len(refs) - 2) // 3
+    came, left = refs[-2], refs[-1]
+    takes = [pltpu.make_async_copy(refs[m], refs[2 * n + m], came.at[m]) for m in range(n)]
+    gives = [pltpu.make_async_copy(refs[2 * n + m], refs[n + m], left.at[m]) for m in range(n)]
+    for copy in takes:
         copy.start()
-    for copy in copies:
+    for take, give in zip(takes, gives):
+        take.wait()
+        give.start()
+    for copy in gives:
         copy.wait()
 
 
@@ -500,7 +505,6 @@
                 ((4, flat, ch), F32),
             ]
         )
-        held = sum(math.prod(shape) * jnp.dtype(kind).itemsize for shape, kind in buffers)
         scratch = [pltpu.VMEM(shape, kind) for shape, kind in buffers]
         n_io = len(ins) + len(results)
         done = pl.pallas_call(
@@ -513,7 +517,7 @@
             + scratch[n_io:]
             + [dma((n,)) for n in (n_ja, n_ja, n_ia, n_ia, n_ja, n_ja, n_ia, n_ia)],
             compiler_params=pltpu.CompilerParams(
-                collective_id=0, has_side_effects=True, vmem_limit_bytes=held + 4 * 1024 * 1024
+                collective_id=0, has_side_effects=True, vmem_limit_bytes=VMEM_BYTES
             ),
         )(*ins)
         update, gslab, gcols, gtile = pl.pallas_call(
@@ -521,7 +525,8 @@
             out_shape=results,
             in_specs=[anywhere] * len(results),
             out_specs=[anywhere] * len(results),
-            scratch_shapes=[dma((len(results),))],
+            scratch_shapes=scratch[len(ins) : n_io] + [dma((len(results),))] * 2,
+            compiler_params=pltpu.CompilerParams(vmem_limit_bytes=VMEM_BYTES),
         )(*done)
         return update, gslab, jnp.transpose(gcols, (1, 0, 2)), gtile
 

time: 61.3 us -> 35.8 us (0.58)
  Pallas kernels: 50.2 us -> 35 us
  local copies, waits for them, and re-layouts: 9.96 us -> 0 us
    pallas_call x1, Pallas kernels: 16.5 us -> 1.81 us  [shards(): pl.pallas_call(move, out_shape=results, in_specs=[anywhere] * len(results...]
    unnamed x32 -> x0, local copies, waits for them, and re-layouts: 9.96 us -> none
where the time goes in v3:
time: 35.8 us; the launch traced here: 35.7 us
  Pallas kernels  35 us (98%)
  between operations  0.64 us (2%)
    pallas_call x1, Pallas kernels, shards(): pl.pallas_call(functools.partial(kernel, n_ia, n_ja), out_shape=results,...  33.2 us
    pallas_call x1, Pallas kernels, shards(): pl.pallas_call(move, out_shape=results, in_specs=[anywhere] * len(results...  1.81 us

profile of v3, /device:TPU:0, one launch (start us, length us, event | category | flops | bytes accessed | tf_op | source)
XLA Modules:
  0.0 35.7 jit_solution(13661154420544807946)
XLA Ops:
  0.6 33.2 %shard_map.147 = (bf16[32,16,128]{2,1,0:T(8,128)(2,1)}, bf16[32,24,128]{2,1,0:T(8,128)(2,1)}, bf16[12,16,128]{2,1,0:T(8,128)(2,1)}, bf16[32,16,128]{2,1,0:T(8,128)(2,1)}) custom-call(bf16[32,24,128]{2,1,0:T(8,128)(2,1)} %slab_hbm.1, bf16[12,16,128]{2,1,0:T(8,128)(2,1)} %bitcast.6, bf16[32,16,128]{2,1,0:T(8,128)(2,1)} %tile_hbm.1, ...), custom_call_target="tpu_custom_call" | custom-call | tf_op jit(solution)/shard_map/pallas_call | solution.py:510
  33.9 1.8 %shard_map.148 = (bf16[32,16,128]{2,1,0:T(8,128)(2,1)}, bf16[32,24,128]{2,1,0:T(8,128)(2,1)}, bf16[12,16,128]{2,1,0:T(8,128)(2,1)}, bf16[32,16,128]{2,1,0:T(8,128)(2,1)}) custom-call(bf16[32,16,128]{2,1,0:T(8,128)(2,1)} %get-tuple-element.12.refs_0_, bf16[32,24,128]{2,1,0:T(8,128)(2,1)} %get-tuple-element.13.refs_1_, ...), custom_call_target="tpu_custom_call" | custom-call | tf_op jit(solution)/shard_map/pallas_call | solution.py:523

commit v4 on v3

--- a/solution.py
+++ b/solution.py
@@ -94,10 +94,14 @@
     lrecv,
     rsend,
     rrecv,
+    fsend,
+    frecv,
     dlsend,
     dlrecv,
     drsend,
     drrecv,
+    sibsend,
+    sibrecv,
 ):
     my_ia, my_ja = lax.axis_index("ia"), lax.axis_index("ja")
     rows_i, k_l, ch = slab_ref.shape
@@ -136,11 +140,22 @@
     for copy in ins:
         copy.start()
 
+    n_z = n_ia // 2
+    my_z, my_core = my_ia // 2, lax.rem(my_ia, 2)
+    sibling = my_z * 2 + 1 - my_core
+    square = n_ja == 4 and k_l % 2 == 0
+    half = k_l // 2
+
     def ja_peer(s):
+        if square:
+            return lax.rem(my_ja // 2 + s // 2, 2) * 2 + lax.rem(my_ja + s, 2)
         return lax.rem(my_ja + s, n_ja)
 
     def ia_peer(s):
         return lax.rem(my_ia + s, n_ia)
+
+    def z_peer(s):
+        return lax.rem(my_z + s, n_z)
 
     barrier = pltpu.get_barrier_semaphore()
 
@@ -201,6 +216,18 @@
             device_id_type=MESH,
         )
 
+    def left_hop(m):
+        owner, part, to = ((0, 0, 1), (0, 1, 2), (0, 1, 1), (0, 0, 2), (1, 0, 2), (2, 1, 1))[m]
+        piece = left_all.at[pl.ds(ja_peer(owner) * k_l + part * half, half)]
+        return pltpu.make_async_remote_copy(
+            src_ref=piece,
+            dst_ref=piece,
+            send_sem=lsend.at[m],
+            recv_sem=lrecv.at[m],
+            device_id=(my_ia, ja_peer(to)),
+            device_id_type=MESH,
+        )
+
     def right_copy(s):
         own = right_all.at[pl.ds(my_ia * k_r, k_r)]
         return pltpu.make_async_remote_copy(
@@ -208,7 +235,18 @@
             dst_ref=own,
             send_sem=rsend.at[s],
             recv_sem=rrecv.at[s],
-            device_id=(ia_peer(s), my_ja),
+            device_id=(z_peer(s) * 2 + my_core, my_ja),
+            device_id_type=MESH,
+        )
+
+    def right_forward(s):
+        piece = right_all.at[pl.ds((z_peer(n_z - s) * 2 + my_core) * k_r, k_r)]
+        return pltpu.make_async_remote_copy(
+            src_ref=piece,
+            dst_ref=piece,
+            send_sem=fsend.at[s],
+            recv_sem=frecv.at[s],
+            device_id=(sibling, my_ja),
             device_id_type=MESH,
         )
 
@@ -223,8 +261,31 @@
             device_id_type=MESH,
         )
 
+    def dl_hop(m):
+        piece, part, to, slot = (
+            (3, 0, 1, 3), (3, 1, 2, 3), (1, 0, 1, 1), (2, 1, 2, 2), (1, 1, 1, 1), (2, 0, 2, 2),
+        )[m]
+        return pltpu.make_async_remote_copy(
+            src_ref=left_all.at[pl.ds(ja_peer(piece) * k_l + part * half, half)],
+            dst_ref=dl_recv.at[slot, pl.ds(part * half, half)],
+            send_sem=dlsend.at[m],
+            recv_sem=dlrecv.at[m],
+            device_id=(my_ia, ja_peer(to)),
+            device_id_type=MESH,
+        )
+
+    def dr_sibling(s):
+        return pltpu.make_async_remote_copy(
+            src_ref=right_all.at[pl.ds((z_peer(s) * 2 + 1 - my_core) * k_r, k_r)],
+            dst_ref=dr_recv.at[n_z + s],
+            send_sem=sibsend.at[s],
+            recv_sem=sibrecv.at[s],
+            device_id=(sibling, my_ja),
+            device_id_type=MESH,
+        )
+
     def dr_copy(s):
-        to = ia_peer(s)
+        to = z_peer(s) * 2 + my_core
         return pltpu.make_async_remote_copy(
             src_ref=right_all.at[pl.ds(to * k_r, k_r)],
             dst_ref=dr_recv.at[s],
@@ -243,7 +304,8 @@
 
     project(cols_piece, rows_j, k_r, wr_ref, save_r, right_all, my_ia * k_r)
     pl.semaphore_wait(barrier, n_ia + n_ja - 2)
-    each(right_copy, n_ia, lambda c: c.start())
+    each(right_copy, n_z, lambda c: c.start())
+    right_forward(0).start()
     for copy in ins[4:6]:
         copy.wait()
 
@@ -253,7 +315,11 @@
 
     lax.fori_loop(0, rows_i, widen, 0, unroll=4)
     project(slab_piece, rows_i, k_l, wl_ref, save_l, left_all, my_ja * k_l)
-    each(left_copy, n_ja, lambda c: c.start())
+    if square:
+        for m in range(4):
+            left_hop(m).start()
+    else:
+        each(left_copy, n_ja, lambda c: c.start())
 
     for copy in ins[6:]:
         copy.wait()
@@ -277,16 +343,46 @@
 
     lax.fori_loop(0, rows_i // t_rows, gate_body, 0)
 
-    each(right_copy, n_ia, lambda c: c.wait())
+    def pass_on(s, c):
+        right_copy(s).wait_recv()
+        right_forward(s).start()
+        return c
+
+    lax.fori_loop(1, n_z, pass_on, 0)
+    if square:
+        left_hop(0).wait_recv()
+        left_hop(4).start()
+        left_hop(1).wait_recv()
+        left_hop(5).start()
+    each(right_copy, n_z, lambda c: c.wait_send())
+    lax.fori_loop(0, n_z, lambda s, c: (right_forward(s).wait(), c)[1], 0)
 
     block = math.gcd(rows_j, 8)
 
     def tri_chunk(s, c):
-        @pl.when(s > 0)
-        def _():
-            left_copy(s).wait()
-
-        k_first = lax.rem(my_ja - s + n_ja, n_ja) * k_l
+        if square:
+
+            @pl.when(s == 1)
+            def _():
+                left_hop(2).wait_recv()
+
+            @pl.when(s == 2)
+            def _():
+                left_hop(3).wait_recv()
+
+            @pl.when(s == 3)
+            def _():
+                left_hop(4).wait_recv()
+                left_hop(5).wait_recv()
+
+            k_first = ja_peer(s) * k_l
+        else:
+
+            @pl.when(s > 0)
+            def _():
+                left_copy(s).wait()
+
+            k_first = ja_peer(n_ja - s) * k_l
 
         def to_f32(k, c):
             left_f[k] = left_all[k].astype(F32)
@@ -311,6 +407,9 @@
 
     tri_t[...] = jnp.zeros_like(tri_t)
     lax.fori_loop(0, n_ja, tri_chunk, 0)
+    if square:
+        for m in range(6):
+            left_hop(m).wait_send()
 
     def tile_body(t, c):
         at = tile_slot(t)
@@ -356,8 +455,8 @@
 
         lax.fori_loop(0, k_l // u_l, body, 0)
 
-    def right_part(s):
-        k_first = ia_peer(s) * k_r
+    def right_part(to, came=None):
+        k_first = to * k_r
         u_r = math.gcd(k_r, 4)
 
         def body(t, c):
@@ -369,39 +468,60 @@
                     term = left_f[k0 + u, pl.ds(i, 1), :] * d
                     accs[u] = term if i == 0 else accs[u] + term
             for u in range(u_r):
-                right_all[k0 + u] = accs[u].astype(BF16)
+                acc = accs[u]
+                if came is not None:
+                    acc = acc + dr_recv[came, t * u_r + u].astype(F32)
+                right_all[k0 + u] = acc.astype(BF16)
             return c
 
         lax.fori_loop(0, k_r // u_r, body, 0)
 
-    groups = min(n_ia, n_ja)
-
-    def group_body(g, c):
-        def one_right(v, c):
-            s = g * (n_ia // groups) + v + 1
-            right_part(s)
-
-            @pl.when(s < n_ia)
-            def _():
-                dr_copy(s).start()
-
-            return c
-
-        def one_left(v, c):
-            s = g * (n_ja // groups) + v + 1
-            left_part(s)
-
-            @pl.when(s < n_ja)
-            def _():
-                dl_copy(s).start()
-
-            return c
-
-        lax.fori_loop(0, n_ia // groups, one_right, 0)
-        lax.fori_loop(0, n_ja // groups, one_left, 0)
-        return c
-
-    lax.fori_loop(0, groups, group_body, 0)
+    def for_sibling(v, c):
+        s = lax.rem(v + 1, n_z)
+        right_part(z_peer(s) * 2 + 1 - my_core)
+        dr_sibling(s).start()
+        return c
+
+    def for_core(s, c):
+        dr_sibling(s).wait_recv()
+        right_part(z_peer(s) * 2 + my_core, n_z + s)
+        dr_copy(s).start()
+        return c
+
+    def for_ja(s, c):
+        left_part(s)
+        dl_copy(s).start()
+        return c
+
+    def add_half(slot, part):
+        at = pl.ds(ja_peer(slot) * k_l + part * half, half)
+        mine = left_all[at].astype(F32)
+        came = dl_recv[3, pl.ds(part * half, half)].astype(F32)
+        left_all[at] = (mine + came).astype(BF16)
+
+    if square:
+        left_part(3)
+        dl_hop(0).start()
+        dl_hop(1).start()
+        lax.fori_loop(0, n_z, for_sibling, 0)
+        left_part(1)
+        dl_hop(2).start()
+        left_part(2)
+        dl_hop(3).start()
+        lax.fori_loop(1, n_z, for_core, 0)
+        dl_hop(0).wait_recv()
+        add_half(2, 0)
+        dl_hop(5).start()
+        dl_hop(1).wait_recv()
+        add_half(1, 1)
+        dl_hop(4).start()
+    else:
+        lax.fori_loop(0, n_z, for_sibling, 0)
+        lax.fori_loop(1, n_z, for_core, 0)
+        lax.fori_loop(1, n_ja, for_ja, 0)
+    left_part(0)
+    dr_sibling(0).wait_recv()
+    right_part(my_ia)
 
     def tile_back(t, c):
         at = tile_slot(t)
@@ -413,7 +533,7 @@
     lax.fori_loop(0, rows_i // t_rows, tile_back, 0)
     outs[1].start()
 
-    def project_back(put, rows, count, w_ref, save, edges, base, recv, n):
+    def project_back(put, rows, count, w_ref, save, edges, base, recv, first, n):
         step = chunk_of(count, rows, 256)
 
         def body(t, c):
@@ -424,7 +544,7 @@
             def add(s, d):
                 return d + recv[s, pl.ds(k0, step)].astype(F32)
 
-            d = lax.fori_loop(1, n, add, d, unroll=n <= 8).reshape(step * rows, ch)
+            d = lax.fori_loop(first, n, add, d, unroll=n <= 8).reshape(step * rows, ch)
             linear, sigma = save[2, at, :], save[3, at, :]
             p = jnp.concatenate([d * sigma, d * linear * sigma * (1.0 - sigma)], axis=-1)
             grad = dot_t(p.astype(BF16), w_ref[...])
@@ -440,11 +560,19 @@
         for u in range(step):
             xs_l[pl.ds(k0 + u, rows_i, stride=pitch), :] = out[u * rows_i : (u + 1) * rows_i]
 
-    each(dr_copy, n_ia, lambda c: c.wait())
-    project_back(put_cols, rows_j, k_r, wr_ref, save_r, right_all, my_ia * k_r, dr_recv, n_ia)
+    each(dr_copy, n_z, lambda c: c.wait())
+    lax.fori_loop(0, n_z, lambda s, c: (dr_sibling(s).wait_send(), c)[1], 0)
+    project_back(put_cols, rows_j, k_r, wr_ref, save_r, right_all, my_ia * k_r, dr_recv, 1, n_z + 1)
     outs[2].start()
-    each(dl_copy, n_ja, lambda c: c.wait())
-    project_back(put_slab, rows_i, k_l, wl_ref, save_l, left_all, my_ja * k_l, dl_recv, n_ja)
+    if square:
+        for m in range(6):
+            dl_hop(m).wait_send()
+        for m in range(2, 6):
+            dl_hop(m).wait_recv()
+    else:
+        each(dl_copy, n_ja, lambda c: c.wait())
+    last = 3 if square else n_ja
+    project_back(put_slab, rows_i, k_l, wl_ref, save_l, left_all, my_ja * k_l, dl_recv, 1, last)
 
     def narrow(r, c):
         gslab_ref[r] = xs_l[pl.ds(pl.multiple_of(r * pitch, 8), k_l), :].astype(BF16)
@@ -515,7 +643,7 @@
             scratch_shapes=scratch[:n_io]
             + [dma((len(ins),)), dma((len(results),))]
             + scratch[n_io:]
-            + [dma((n,)) for n in (n_ja, n_ja, n_ia, n_ia, n_ja, n_ja, n_ia, n_ia)],
+            + [dma((n,)) for n in (n_ja + 2, n_ja + 2, n_ia, n_ia, n_ia, n_ia) * 2],
             compiler_params=pltpu.CompilerParams(
                 collective_id=0, has_side_effects=True, vmem_limit_bytes=VMEM_BYTES
             ),

time: 35.8 us -> 31.5 us (0.88)
  Pallas kernels: 35 us -> 30.7 us
    pallas_call x1, Pallas kernels: 33.2 us -> 28.9 us  [shards(): pl.pallas_call(functools.partial(kernel, n_ia, n_ja), out_shape=results,...]
where the time goes in v4:
time: 31.5 us; the launch traced here: 31.4 us
  Pallas kernels  30.7 us (97%)
  between operations  0.64 us (2%)
    pallas_call x1, Pallas kernels, shards(): pl.pallas_call(functools.partial(kernel, n_ia, n_ja), out_shape=results,...  28.9 us
    pallas_call x1, Pallas kernels, shards(): pl.pallas_call(move, out_shape=results, in_specs=[anywhere] * len(results...  1.81 us

profile of v4, /device:TPU:0, one launch (start us, length us, event | category | flops | bytes accessed | tf_op | source)
XLA Modules:
  0.0 31.4 jit_solution(14136502399444394742)
XLA Ops:
  0.6 28.9 %shard_map.147 = (bf16[32,16,128]{2,1,0:T(8,128)(2,1)}, bf16[32,24,128]{2,1,0:T(8,128)(2,1)}, bf16[12,16,128]{2,1,0:T(8,128)(2,1)}, bf16[32,16,128]{2,1,0:T(8,128)(2,1)}) custom-call(bf16[32,24,128]{2,1,0:T(8,128)(2,1)} %slab_hbm.1, bf16[12,16,128]{2,1,0:T(8,128)(2,1)} %bitcast.6, bf16[32,16,128]{2,1,0:T(8,128)(2,1)} %tile_hbm.1, ...), custom_call_target="tpu_custom_call" | custom-call | tf_op jit(solution)/shard_map/pallas_call | solution.py:638
  29.6 1.8 %shard_map.148 = (bf16[32,16,128]{2,1,0:T(8,128)(2,1)}, bf16[32,24,128]{2,1,0:T(8,128)(2,1)}, bf16[12,16,128]{2,1,0:T(8,128)(2,1)}, bf16[32,16,128]{2,1,0:T(8,128)(2,1)}) custom-call(bf16[32,16,128]{2,1,0:T(8,128)(2,1)} %get-tuple-element.12.refs_0_, bf16[32,24,128]{2,1,0:T(8,128)(2,1)} %get-tuple-element.13.refs_1_, ...), custom_call_target="tpu_custom_call" | custom-call | tf_op jit(solution)/shard_map/pallas_call | solution.py:651

commit v5 on v4

--- a/solution.py
+++ b/solution.py
@@ -56,10 +56,10 @@
     bias_hbm,
     ugain_hbm,
     ubias_hbm,
-    update_hbm,
-    gslab_hbm,
-    gcols_hbm,
-    gtile_hbm,
+    update_ref,
+    gslab_ref,
+    gcols_ref,
+    gtile_ref,
     slab_ref,
     cols_ref,
     tile_ref,
@@ -72,12 +72,7 @@
     bias_ref,
     ugain_ref,
     ubias_ref,
-    update_ref,
-    gslab_ref,
-    gcols_ref,
-    gtile_ref,
     in_sem,
-    out_sem,
     xs_l,
     save_l,
     save_r,
@@ -126,25 +121,14 @@
             ]
         )
     ]
-    outs = [
-        pltpu.make_async_copy(a, b, out_sem.at[n])
-        for n, (a, b) in enumerate(
-            [
-                (update_ref, update_hbm),
-                (gtile_ref, gtile_hbm),
-                (gcols_ref, gcols_hbm),
-                (gslab_ref, gslab_hbm),
-            ]
-        )
-    ]
     for copy in ins:
         copy.start()
 
     n_z = n_ia // 2
     my_z, my_core = my_ia // 2, lax.rem(my_ia, 2)
     sibling = my_z * 2 + 1 - my_core
-    square = n_ja == 4 and k_l % 2 == 0
-    half = k_l // 2
+    square = n_ja == 4 and k_l % 4 == 0
+    quarter = k_l // 4
 
     def ja_peer(s):
         if square:
@@ -184,11 +168,11 @@
     def cols_piece(k0, step):
         return cols_ref[pl.ds(k0, step)].astype(F32).reshape(step * rows_j, ch)
 
-    def project(piece, rows, count, w_ref, save, edges, base):
+    def project(piece, rows, start, count, w_ref, save, edges, base):
         step = chunk_of(count, rows, 256)
 
         def body(t, c):
-            k0 = t * step
+            k0 = start + t * step
             x = piece(k0, step)
             scaled, inverse = normalize(x)
             q = dot((scaled * gain + bias).astype(BF16), w_ref[...])
@@ -216,17 +200,21 @@
             device_id_type=MESH,
         )
 
-    def left_hop(m):
-        owner, part, to = ((0, 0, 1), (0, 1, 2), (0, 1, 1), (0, 0, 2), (1, 0, 2), (2, 1, 1))[m]
-        piece = left_all.at[pl.ds(ja_peer(owner) * k_l + part * half, half)]
+    def left_hop(owner, q, to, sem):
+        piece = left_all.at[pl.ds(ja_peer(owner) * k_l + q * quarter, quarter)]
         return pltpu.make_async_remote_copy(
             src_ref=piece,
             dst_ref=piece,
-            send_sem=lsend.at[m],
-            recv_sem=lrecv.at[m],
+            send_sem=lsend.at[sem],
+            recv_sem=lrecv.at[sem],
             device_id=(my_ia, ja_peer(to)),
             device_id_type=MESH,
         )
+
+    def own_hop(to, q):
+        return left_hop(0, q, to, (to - 1) * 4 + q)
+
+    relays = [left_hop(2 - (q + 1) % 2, q, 2 - q % 2, 8 + q) for q in range(4 * square)]
 
     def right_copy(s):
         own = right_all.at[pl.ds(my_ia * k_r, k_r)]
@@ -261,18 +249,21 @@
             device_id_type=MESH,
         )
 
-    def dl_hop(m):
-        piece, part, to, slot = (
-            (3, 0, 1, 3), (3, 1, 2, 3), (1, 0, 1, 1), (2, 1, 2, 2), (1, 1, 1, 1), (2, 0, 2, 2),
-        )[m]
-        return pltpu.make_async_remote_copy(
-            src_ref=left_all.at[pl.ds(ja_peer(piece) * k_l + part * half, half)],
-            dst_ref=dl_recv.at[slot, pl.ds(part * half, half)],
-            send_sem=dlsend.at[m],
-            recv_sem=dlrecv.at[m],
+    def dl_hop(piece, q, to, slot, sem):
+        return pltpu.make_async_remote_copy(
+            src_ref=left_all.at[pl.ds(ja_peer(piece) * k_l + q * quarter, quarter)],
+            dst_ref=dl_recv.at[slot, pl.ds(q * quarter, quarter)],
+            send_sem=dlsend.at[sem],
+            recv_sem=dlrecv.at[sem],
             device_id=(my_ia, ja_peer(to)),
             device_id_type=MESH,
         )
+
+    def across_hop(q):
+        return dl_hop(3, q, 1 + q % 2, 3, q)
+
+    def near_hop(to, q):
+        return dl_hop(to, q, to, to, to * 4 + q)
 
     def dr_sibling(s):
         return pltpu.make_async_remote_copy(
@@ -302,7 +293,7 @@
 
         lax.fori_loop(1, n, body, 0)
 
-    project(cols_piece, rows_j, k_r, wr_ref, save_r, right_all, my_ia * k_r)
+    project(cols_piece, rows_j, 0, k_r, wr_ref, save_r, right_all, my_ia * k_r)
     pl.semaphore_wait(barrier, n_ia + n_ja - 2)
     each(right_copy, n_z, lambda c: c.start())
     right_forward(0).start()
@@ -314,11 +305,20 @@
         return c
 
     lax.fori_loop(0, rows_i, widen, 0, unroll=4)
-    project(slab_piece, rows_i, k_l, wl_ref, save_l, left_all, my_ja * k_l)
+    def project_slab(start, count):
+        project(slab_piece, rows_i, start, count, wl_ref, save_l, left_all, my_ja * k_l)
+
     if square:
-        for m in range(4):
-            left_hop(m).start()
+
+        def send_quarter(q, c):
+            project_slab(q * quarter, quarter)
+            own_hop(1, q).start()
+            own_hop(2, q).start()
+            return c
+
+        lax.fori_loop(0, 4, send_quarter, 0)
     else:
+        project_slab(0, k_l)
         each(left_copy, n_ja, lambda c: c.start())
 
     for copy in ins[6:]:
@@ -348,12 +348,17 @@
         right_forward(s).start()
         return c
 
+    def relay(q):
+        own_hop(2 - (q + 1) % 2, q).wait_recv()
+        relays[q].start()
+
+    if square:
+        relay(0)
+        relay(1)
     lax.fori_loop(1, n_z, pass_on, 0)
     if square:
-        left_hop(0).wait_recv()
-        left_hop(4).start()
-        left_hop(1).wait_recv()
-        left_hop(5).start()
+        relay(2)
+        relay(3)
     each(right_copy, n_z, lambda c: c.wait_send())
     lax.fori_loop(0, n_z, lambda s, c: (right_forward(s).wait(), c)[1], 0)
 
@@ -364,16 +369,18 @@
 
             @pl.when(s == 1)
             def _():
-                left_hop(2).wait_recv()
+                own_hop(1, 1).wait_recv()
+                own_hop(1, 3).wait_recv()
 
             @pl.when(s == 2)
             def _():
-                left_hop(3).wait_recv()
+                own_hop(2, 0).wait_recv()
+                own_hop(2, 2).wait_recv()
 
             @pl.when(s == 3)
             def _():
-                left_hop(4).wait_recv()
-                left_hop(5).wait_recv()
+                for copy in relays:
+                    copy.wait_recv()
 
             k_first = ja_peer(s) * k_l
         else:
@@ -408,8 +415,10 @@
     tri_t[...] = jnp.zeros_like(tri_t)
     lax.fori_loop(0, n_ja, tri_chunk, 0)
     if square:
-        for m in range(6):
-            left_hop(m).wait_send()
+        for q in range(4):
+            own_hop(1, q).wait_send()
+            own_hop(2, q).wait_send()
+            relays[q].wait_send()
 
     def tile_body(t, c):
         at = tile_slot(t)
@@ -435,11 +444,10 @@
         return c
 
     lax.fori_loop(0, rows_i // t_rows, tile_body, 0)
-    outs[0].start()
-
-    def left_part(s):
-        k_first = ja_peer(s) * k_l
-        u_l = math.gcd(k_l, 4)
+
+    def left_part(s, start=0, count=k_l):
+        k_first = ja_peer(s) * k_l + start
+        u_l = chunk_of(count, 1, 4)
 
         def body(t, c):
             k0 = k_first + t * u_l
@@ -453,7 +461,7 @@
                 left_all[k0 + u] = accs[u].astype(BF16)
             return c
 
-        lax.fori_loop(0, k_l // u_l, body, 0)
+        lax.fori_loop(0, count // u_l, body, 0)
 
     def right_part(to, came=None):
         k_first = to * k_r
@@ -493,28 +501,31 @@
         dl_copy(s).start()
         return c
 
-    def add_half(slot, part):
-        at = pl.ds(ja_peer(slot) * k_l + part * half, half)
-        mine = left_all[at].astype(F32)
-        came = dl_recv[3, pl.ds(part * half, half)].astype(F32)
-        left_all[at] = (mine + came).astype(BF16)
+    def across(q, c):
+        left_part(3, q * quarter, quarter)
+        across_hop(q).start()
+        return c
+
+    def add_across(q):
+        across_hop(q).wait_recv()
+        to = 2 - q % 2
+        at = pl.ds(ja_peer(to) * k_l + q * quarter, quarter)
+        came = dl_recv[3, pl.ds(q * quarter, quarter)].astype(F32)
+        left_all[at] = (left_all[at].astype(F32) + came).astype(BF16)
+        near_hop(to, q).start()
 
     if square:
-        left_part(3)
-        dl_hop(0).start()
-        dl_hop(1).start()
+        lax.fori_loop(0, 4, across, 0)
         lax.fori_loop(0, n_z, for_sibling, 0)
         left_part(1)
-        dl_hop(2).start()
+        near_hop(1, 0).start()
+        near_hop(1, 2).start()
         left_part(2)
-        dl_hop(3).start()
+        near_hop(2, 1).start()
+        near_hop(2, 3).start()
         lax.fori_loop(1, n_z, for_core, 0)
-        dl_hop(0).wait_recv()
-        add_half(2, 0)
-        dl_hop(5).start()
-        dl_hop(1).wait_recv()
-        add_half(1, 1)
-        dl_hop(4).start()
+        for q in range(4):
+            add_across(q)
     else:
         lax.fori_loop(0, n_z, for_sibling, 0)
         lax.fori_loop(1, n_z, for_core, 0)
@@ -531,13 +542,12 @@
         return c
 
     lax.fori_loop(0, rows_i // t_rows, tile_back, 0)
-    outs[1].start()
-
-    def project_back(put, rows, count, w_ref, save, edges, base, recv, first, n):
+
+    def project_back(put, rows, start, count, w_ref, save, edges, base, recv, first, n):
         step = chunk_of(count, rows, 256)
 
         def body(t, c):
-            k0 = t * step
+            k0 = start + t * step
             at = pl.ds(pl.multiple_of(k0 * rows, 8), step * rows)
             d = edges[pl.ds(base + k0, step)].astype(F32)
 
@@ -562,39 +572,44 @@
 
     each(dr_copy, n_z, lambda c: c.wait())
     lax.fori_loop(0, n_z, lambda s, c: (dr_sibling(s).wait_send(), c)[1], 0)
-    project_back(put_cols, rows_j, k_r, wr_ref, save_r, right_all, my_ia * k_r, dr_recv, 1, n_z + 1)
-    outs[2].start()
+    project_back(
+        put_cols, rows_j, 0, k_r, wr_ref, save_r, right_all, my_ia * k_r, dr_recv, 1, n_z + 1
+    )
+    def back_slab(start, count, last):
+        project_back(
+            put_slab, rows_i, start, count, wl_ref, save_l, left_all, my_ja * k_l, dl_recv, 1, last
+        )
+
     if square:
-        for m in range(6):
-            dl_hop(m).wait_send()
-        for m in range(2, 6):
-            dl_hop(m).wait_recv()
+
+        def back_quarter(q, c):
+            near_hop(1, q).wait_recv()
+            near_hop(2, q).wait_recv()
+            back_slab(q * quarter, quarter, 3)
+            return c
+
+        lax.fori_loop(0, 4, back_quarter, 0)
+        for q in range(4):
+            across_hop(q).wait_send()
+            near_hop(1, q).wait_send()
+            near_hop(2, q).wait_send()
     else:
         each(dl_copy, n_ja, lambda c: c.wait())
-    last = 3 if square else n_ja
-    project_back(put_slab, rows_i, k_l, wl_ref, save_l, left_all, my_ja * k_l, dl_recv, 1, last)
+        back_slab(0, k_l, n_ja)
 
     def narrow(r, c):
         gslab_ref[r] = xs_l[pl.ds(pl.multiple_of(r * pitch, 8), k_l), :].astype(BF16)
         return c
 
     lax.fori_loop(0, rows_i, narrow, 0, unroll=4)
-    outs[3].start()
-    for copy in outs:
-        copy.wait()
 
 
 def move(*refs):
-    n = (len(refs) - 2) // 3
-    came, left = refs[-2], refs[-1]
-    takes = [pltpu.make_async_copy(refs[m], refs[2 * n + m], came.at[m]) for m in range(n)]
-    gives = [pltpu.make_async_copy(refs[2 * n + m], refs[n + m], left.at[m]) for m in range(n)]
-    for copy in takes:
+    n = len(refs) // 2
+    copies = [pltpu.make_async_copy(refs[m], refs[n + m], refs[-1].at[m]) for m in range(n)]
+    for copy in copies:
         copy.start()
-    for take, give in zip(takes, gives):
-        take.wait()
-        give.start()
-    for copy in gives:
+    for copy in copies:
         copy.wait()
 
 
@@ -617,7 +632,6 @@
         results = [jax.ShapeDtypeStruct(a.shape, BF16) for a in (tile, slab, cols, tile)]
         buffers = (
             [(a.shape, a.dtype) for a in ins]
-            + [(a.shape, a.dtype) for a in results]
             + [
                 ((rows_i * pitch, ch), F32),
                 ((4, rows_i * k_l, ch), F32),
@@ -634,16 +648,16 @@
             ]
         )
         scratch = [pltpu.VMEM(shape, kind) for shape, kind in buffers]
-        n_io = len(ins) + len(results)
+        vmem = pl.BlockSpec(memory_space=pltpu.VMEM)
         done = pl.pallas_call(
             functools.partial(kernel, n_ia, n_ja),
-            out_shape=results,
+            out_shape=[pltpu.VMEM(a.shape, a.dtype) for a in results],
             in_specs=[pl.BlockSpec(memory_space=pltpu.HBM)] * len(ins),
-            out_specs=[anywhere] * len(results),
-            scratch_shapes=scratch[:n_io]
-            + [dma((len(ins),)), dma((len(results),))]
-            + scratch[n_io:]
-            + [dma((n,)) for n in (n_ja + 2, n_ja + 2, n_ia, n_ia, n_ia, n_ia) * 2],
+            out_specs=[vmem] * len(results),
+            scratch_shapes=scratch[: len(ins)]
+            + [dma((len(ins),))]
+            + scratch[len(ins) :]
+            + [dma((n,)) for n in (n_ja + 8, n_ja + 8, n_ia, n_ia, n_ia, n_ia) * 2],
             compiler_params=pltpu.CompilerParams(
                 collective_id=0, has_side_effects=True, vmem_limit_bytes=VMEM_BYTES
             ),
@@ -651,11 +665,11 @@
         update, gslab, gcols, gtile = pl.pallas_call(
             move,
             out_shape=results,
-            in_specs=[anywhere] * len(results),
+            in_specs=[vmem] * len(results),
             out_specs=[anywhere] * len(results),
-            scratch_shapes=scratch[len(ins) : n_io] + [dma((len(results),))] * 2,
+            scratch_shapes=[dma((len(results),))],
             compiler_params=pltpu.CompilerParams(vmem_limit_bytes=VMEM_BYTES),
-        )(*done)
+        )(*[pltpu.with_memory_space_constraint(a, pltpu.VMEM) for a in done])
         return update, gslab, jnp.transpose(gcols, (1, 0, 2)), gtile
 
     return jax.shard_map(

time: 31.5 us -> 30.7 us (0.975)
  Pallas kernels: 30.7 us -> 29.9 us
    pallas_call x2, Pallas kernels: 30.7 us -> 29.9 us  [the longest x1 29 us: shards(): pl.pallas_call(functools.partial(kernel, n_ia, n_ja), out_shape=[pltpu.VM...]
where the time goes in v5:
time: 30.7 us; the launch traced here: 30.5 us
  Pallas kernels  29.9 us (97%)
  between operations  0.64 us (2%)
    pallas_call x1, Pallas kernels, shards(): pl.pallas_call(functools.partial(kernel, n_ia, n_ja), out_shape=[pltpu.VM...  29 us
    pallas_call x1, Pallas kernels, shards(): pl.pallas_call(move, out_shape=results, in_specs=[vmem] * len(results), o...  0.82 us

profile of v5, /device:TPU:0, one launch (start us, length us, event | category | flops | bytes accessed | tf_op | source)
XLA Modules:
  0.0 30.5 jit_solution(14718292641079353484)
XLA Ops:
  0.6 29.0 %shard_map.147 = (bf16[32,16,128]{2,1,0:T(8,128)(2,1)S(1)}, bf16[32,24,128]{2,1,0:T(8,128)(2,1)S(1)}, bf16[12,16,128]{2,1,0:T(8,128)(2,1)S(1)}, bf16[32,16,128]{2,1,0:T(8,128)(2,1)S(1)}) custom-call(bf16[32,24,128]{2,1,0:T(8,128)(2,1)} %slab_hbm.1, bf16[12,16,128]{2,1,0:T(8,128)(2,1)} %bitcast.6, bf16[32,16,128]{2,1,0:T(8,128)(2,1)} %tile_hbm.1, ...), custom_call_target="tpu_custom_call" | custom-call | tf_op jit(solution)/shard_map/pallas_call | solution.py:652
  29.7 0.8 %shard_map.148 = (bf16[32,16,128]{2,1,0:T(8,128)(2,1)}, bf16[32,24,128]{2,1,0:T(8,128)(2,1)}, bf16[12,16,128]{2,1,0:T(8,128)(2,1)}, bf16[32,16,128]{2,1,0:T(8,128)(2,1)}) custom-call(bf16[32,16,128]{2,1,0:T(8,128)(2,1)S(1)} %get-tuple-element.12.refs_0_, bf16[32,24,128]{2,1,0:T(8,128)(2,1)S(1)} %get-tuple-element.13.refs_1_, ...), custom_call_target="tpu_custom_call" | custom-call | tf_op jit(solution)/shard_map/pallas_call | solution.py:665

commit v6 on v5

--- a/solution.py
+++ b/solution.py
@@ -321,39 +321,43 @@
         project_slab(0, k_l)
         each(left_copy, n_ja, lambda c: c.start())
 
+    def pass_on(s, c):
+        right_copy(s).wait_recv()
+        right_forward(s).start()
+        return c
+
+    def relay(q):
+        own_hop(2 - (q + 1) % 2, q).wait_recv()
+        relays[q].start()
+
+    if square:
+        relay(0)
+
     for copy in ins[6:]:
         copy.wait()
     ugain = ugain_ref[...]
     ubias = ubias_ref[...]
-    t_rows = chunk_of(rows_i, rows_j, 128)
+    t_rows = chunk_of(rows_i, rows_j, 512)
     t_flat = t_rows * rows_j
 
-    def tile_slot(t):
-        return pl.ds(pl.multiple_of(t * t_flat, 8), t_flat)
+    def by_j(i):
+        return pl.ds(i, rows_j, stride=rows_i)
 
     def gate_body(t, c):
         x = tile_ref[pl.ds(t * t_rows, t_rows)].astype(F32).reshape(t_flat, ch)
         scaled, inverse = normalize(x)
         gate = jax.nn.sigmoid(dot((scaled * gain + bias).astype(BF16), wg_ref[...]))
-        at = tile_slot(t)
+        at = pl.ds(pl.multiple_of(t * t_flat, 8), t_flat)
         save_t[0, at, :] = scaled
         save_t[1, at, :] = jnp.broadcast_to(inverse, scaled.shape)
-        save_t[2, at, :] = gate
+        for u in range(t_rows):
+            save_t[2, by_j(t * t_rows + u), :] = gate[u * rows_j : (u + 1) * rows_j]
+            save_t[3, by_j(t * t_rows + u), :] = cot_ref[t * t_rows + u].astype(F32)
         return c
 
     lax.fori_loop(0, rows_i // t_rows, gate_body, 0)
 
-    def pass_on(s, c):
-        right_copy(s).wait_recv()
-        right_forward(s).start()
-        return c
-
-    def relay(q):
-        own_hop(2 - (q + 1) % 2, q).wait_recv()
-        relays[q].start()
-
     if square:
-        relay(0)
         relay(1)
     lax.fori_loop(1, n_z, pass_on, 0)
     if square:
@@ -420,30 +424,22 @@
             own_hop(2, q).wait_send()
             relays[q].wait_send()
 
+    j_rows = chunk_of(rows_j, rows_i, 512)
+
     def tile_body(t, c):
-        at = tile_slot(t)
-        tri = jnp.concatenate(
-            [tri_t[pl.ds(t * t_rows + u, rows_j, stride=rows_i), :] for u in range(t_rows)], axis=0
-        )
-        scaled, inverse = normalize(tri)
+        at = pl.ds(pl.multiple_of(t * j_rows * rows_i, 8), j_rows * rows_i)
+        scaled, inverse = normalize(tri_t[at, :])
         outer = dot((scaled * ugain + ubias).astype(BF16), wo_ref[...])
-        gate = save_t[2, at, :]
-        update_ref[pl.ds(t * t_rows, t_rows)] = (
-            (gate * outer).astype(BF16).reshape(t_rows, rows_j, ch)
-        )
-        cot = cot_ref[pl.ds(t * t_rows, t_rows)].astype(F32).reshape(t_flat, ch)
+        gate, cot = save_t[2, at, :], save_t[3, at, :]
         d_outer = (cot * gate).astype(BF16)
-        save_t[3, at, :] = cot * outer * gate * (1.0 - gate)
         d_tri = norm_back(scaled, inverse, dot_t(d_outer, wo_ref[...]), ugain)
-        d_tri = d_tri.astype(BF16).astype(F32)
-        dtri[at, :] = d_tri
-        for u in range(t_rows):
-            tri_t[pl.ds(t * t_rows + u, rows_j, stride=rows_i), :] = d_tri[
-                u * rows_j : (u + 1) * rows_j
-            ]
-        return c
-
-    lax.fori_loop(0, rows_i // t_rows, tile_body, 0)
+        tri_t[at, :] = d_tri.astype(BF16).astype(F32)
+        update = gate * outer
+        save_t[2, at, :] = update
+        save_t[3, at, :] = cot * update * (1.0 - gate)
+        return c
+
+    lax.fori_loop(0, rows_j // j_rows, tile_body, 0)
 
     def left_part(s, start=0, count=k_l):
         k_first = ja_peer(s) * k_l + start
@@ -514,8 +510,13 @@
         left_all[at] = (left_all[at].astype(F32) + came).astype(BF16)
         near_hop(to, q).start()
 
+    def reorder(i, c):
+        dtri[pl.ds(pl.multiple_of(i * rows_j, 8), rows_j), :] = tri_t[by_j(i), :]
+        return c
+
     if square:
         lax.fori_loop(0, 4, across, 0)
+        lax.fori_loop(0, rows_i, reorder, 0, unroll=8)
         lax.fori_loop(0, n_z, for_sibling, 0)
         left_part(1)
         near_hop(1, 0).start()
@@ -527,6 +528,7 @@
         for q in range(4):
             add_across(q)
     else:
+        lax.fori_loop(0, rows_i, reorder, 0, unroll=8)
         lax.fori_loop(0, n_z, for_sibling, 0)
         lax.fori_loop(1, n_z, for_core, 0)
         lax.fori_loop(1, n_ja, for_ja, 0)
@@ -535,16 +537,20 @@
     right_part(my_ia)
 
     def tile_back(t, c):
-        at = tile_slot(t)
-        grad = dot_t(save_t[3, at, :].astype(BF16), wg_ref[...])
+        at = pl.ds(pl.multiple_of(t * t_flat, 8), t_flat)
+        first = t * t_rows
+        for u in range(t_rows):
+            update_ref[first + u] = save_t[2, by_j(first + u), :].astype(BF16)
+        d_gate = jnp.concatenate([save_t[3, by_j(first + u), :] for u in range(t_rows)], axis=0)
+        grad = dot_t(d_gate.astype(BF16), wg_ref[...])
         out = norm_back(save_t[0, at, :], save_t[1, at, :], grad, gain)
-        gtile_ref[pl.ds(t * t_rows, t_rows)] = out.astype(BF16).reshape(t_rows, rows_j, ch)
+        gtile_ref[pl.ds(first, t_rows)] = out.astype(BF16).reshape(t_rows, rows_j, ch)
         return c
 
     lax.fori_loop(0, rows_i // t_rows, tile_back, 0)
 
     def project_back(put, rows, start, count, w_ref, save, edges, base, recv, first, n):
-        step = chunk_of(count, rows, 256)
+        step = chunk_of(count, rows, 512)
 
         def body(t, c):
             k0 = start + t * step
@@ -582,13 +588,14 @@
 
     if square:
 
-        def back_quarter(q, c):
-            near_hop(1, q).wait_recv()
-            near_hop(2, q).wait_recv()
-            back_slab(q * quarter, quarter, 3)
-            return c
-
-        lax.fori_loop(0, 4, back_quarter, 0)
+        def back_half(h, c):
+            for q in (h * 2, h * 2 + 1):
+                near_hop(1, q).wait_recv()
+                near_hop(2, q).wait_recv()
+            back_slab(h * 2 * quarter, 2 * quarter, 3)
+            return c
+
+        lax.fori_loop(0, 2, back_half, 0)
         for q in range(4):
             across_hop(q).wait_send()
             near_hop(1, q).wait_send()

time: 30.7 us -> 29.4 us (0.958)
  Pallas kernels: 29.9 us -> 28.6 us
    pallas_call x1, Pallas kernels: 29 us -> 27.8 us  [shards(): pl.pallas_call(functools.partial(kernel, n_ia, n_ja), out_shape=[pltpu.VM...]
where the time goes in v6:
time: 29.4 us; the launch traced here: 29.3 us
  Pallas kernels  28.6 us (97%)
  between operations  0.64 us (2%)
    pallas_call x1, Pallas kernels, shards(): pl.pallas_call(functools.partial(kernel, n_ia, n_ja), out_shape=[pltpu.VM...  27.8 us
    pallas_call x1, Pallas kernels, shards(): pl.pallas_call(move, out_shape=results, in_specs=[vmem] * len(results), o...  0.82 us

profile of v6, /device:TPU:0, one launch (start us, length us, event | category | flops | bytes accessed | tf_op | source)
XLA Modules:
  0.0 29.3 jit_solution(14714444549188482826)
XLA Ops:
  0.6 27.8 %shard_map.147 = (bf16[32,16,128]{2,1,0:T(8,128)(2,1)S(1)}, bf16[32,24,128]{2,1,0:T(8,128)(2,1)S(1)}, bf16[12,16,128]{2,1,0:T(8,128)(2,1)S(1)}, bf16[32,16,128]{2,1,0:T(8,128)(2,1)S(1)}) custom-call(bf16[32,24,128]{2,1,0:T(8,128)(2,1)} %slab_hbm.1, bf16[12,16,128]{2,1,0:T(8,128)(2,1)} %bitcast.6, bf16[32,16,128]{2,1,0:T(8,128)(2,1)} %tile_hbm.1, ...), custom_call_target="tpu_custom_call" | custom-call | tf_op jit(solution)/shard_map/pallas_call | solution.py:659
  28.4 0.8 %shard_map.148 = (bf16[32,16,128]{2,1,0:T(8,128)(2,1)}, bf16[32,24,128]{2,1,0:T(8,128)(2,1)}, bf16[12,16,128]{2,1,0:T(8,128)(2,1)}, bf16[32,16,128]{2,1,0:T(8,128)(2,1)}) custom-call(bf16[32,16,128]{2,1,0:T(8,128)(2,1)S(1)} %get-tuple-element.12.refs_0_, bf16[32,24,128]{2,1,0:T(8,128)(2,1)S(1)} %get-tuple-element.13.refs_1_, ...), custom_call_target="tpu_custom_call" | custom-call | tf_op jit(solution)/shard_map/pallas_call | solution.py:672

commit v7 on v6

--- a/solution.py
+++ b/solution.py
@@ -395,12 +395,9 @@
 
             k_first = ja_peer(n_ja - s) * k_l
 
-        def to_f32(k, c):
-            left_f[k] = left_all[k].astype(F32)
-            right_f[k] = right_all[k].astype(F32)
-            return c
-
-        lax.fori_loop(k_first, k_first + k_l, to_f32, 0)
+        ks = pl.ds(k_first, k_l)
+        left_f[ks] = left_all[ks].astype(F32)
+        right_f[ks] = right_all[ks].astype(F32)
         for first in range(0, rows_j, block):
 
             def tri_body(k, accs, first=first):
@@ -521,10 +518,10 @@
         left_part(1)
         near_hop(1, 0).start()
         near_hop(1, 2).start()
+        lax.fori_loop(1, n_z, for_core, 0)
         left_part(2)
         near_hop(2, 1).start()
         near_hop(2, 3).start()
-        lax.fori_loop(1, n_z, for_core, 0)
         for q in range(4):
             add_across(q)
     else:
@@ -576,11 +573,6 @@
         for u in range(step):
             xs_l[pl.ds(k0 + u, rows_i, stride=pitch), :] = out[u * rows_i : (u + 1) * rows_i]
 
-    each(dr_copy, n_z, lambda c: c.wait())
-    lax.fori_loop(0, n_z, lambda s, c: (dr_sibling(s).wait_send(), c)[1], 0)
-    project_back(
-        put_cols, rows_j, 0, k_r, wr_ref, save_r, right_all, my_ia * k_r, dr_recv, 1, n_z + 1
-    )
     def back_slab(start, count, last):
         project_back(
             put_slab, rows_i, start, count, wl_ref, save_l, left_all, my_ja * k_l, dl_recv, 1, last
@@ -609,6 +601,12 @@
         return c
 
     lax.fori_loop(0, rows_i, narrow, 0, unroll=4)
+
+    each(dr_copy, n_z, lambda c: c.wait())
+    lax.fori_loop(0, n_z, lambda s, c: (dr_sibling(s).wait_send(), c)[1], 0)
+    project_back(
+        put_cols, rows_j, 0, k_r, wr_ref, save_r, right_all, my_ia * k_r, dr_recv, 1, n_z + 1
+    )
 
 
 def move(*refs):

time: 29.4 us -> 30.2 us (1.027)
  Pallas kernels: 28.6 us -> 29.4 us
    pallas_call x1, Pallas kernels: 27.8 us -> 28.6 us  [shards(): pl.pallas_call(functools.partial(kernel, n_ia, n_ja), out_shape=[pltpu.VM...]
where the time goes in v7:
time: 30.2 us; the launch traced here: 30.1 us
  Pallas kernels  29.4 us (97%)
  between operations  0.64 us (2%)
    pallas_call x1, Pallas kernels, shards(): pl.pallas_call(functools.partial(kernel, n_ia, n_ja), out_shape=[pltpu.VM...  28.6 us
    pallas_call x1, Pallas kernels, shards(): pl.pallas_call(move, out_shape=results, in_specs=[vmem] * len(results), o...  0.82 us

profile of v7, /device:TPU:0, one launch (start us, length us, event | category | flops | bytes accessed | tf_op | source)
XLA Modules:
  0.0 30.1 jit_solution(1525880764076563666)
XLA Ops:
  0.6 28.6 %shard_map.147 = (bf16[32,16,128]{2,1,0:T(8,128)(2,1)S(1)}, bf16[32,24,128]{2,1,0:T(8,128)(2,1)S(1)}, bf16[12,16,128]{2,1,0:T(8,128)(2,1)S(1)}, bf16[32,16,128]{2,1,0:T(8,128)(2,1)S(1)}) custom-call(bf16[32,24,128]{2,1,0:T(8,128)(2,1)} %slab_hbm.1, bf16[12,16,128]{2,1,0:T(8,128)(2,1)} %bitcast.6, bf16[32,16,128]{2,1,0:T(8,128)(2,1)} %tile_hbm.1, ...), custom_call_target="tpu_custom_call" | custom-call | tf_op jit(solution)/shard_map/pallas_call | solution.py:657
  29.2 0.8 %shard_map.148 = (bf16[32,16,128]{2,1,0:T(8,128)(2,1)}, bf16[32,24,128]{2,1,0:T(8,128)(2,1)}, bf16[12,16,128]{2,1,0:T(8,128)(2,1)}, bf16[32,16,128]{2,1,0:T(8,128)(2,1)}) custom-call(bf16[32,16,128]{2,1,0:T(8,128)(2,1)S(1)} %get-tuple-element.12.refs_0_, bf16[32,24,128]{2,1,0:T(8,128)(2,1)S(1)} %get-tuple-element.13.refs_1_, ...), custom_call_target="tpu_custom_call" | custom-call | tf_op jit(solution)/shard_map/pallas_call | solution.py:670
